TPU v7x, 32 devices: a whole 2x2x4 slice. The times are simulated.
32 devices in a mesh: dp: 8 (over z, x), cond: 4 (over y, core).
Axes of the slice: x: 2, y: 2, z: 4, core: 2. Of those that a mesh axis runs over, the one named last changes fastest.
Arguments:
- actions: float32 [4096, 256], P('dp'), may hold values from -6 to 6
- memory: bfloat16 [256, 800, 256], P('dp', 'cond'), may hold values from -6 to 6
- patch_flags: int32 [256, 4], P('dp', 'cond'), may hold values from 49 to 196, as said below
- memory_mask: int32 [256, 800], P('dp', 'cond'), may hold values 0 or 1
- cotangent: float32 [4096, 256], P('dp'), may hold values from -6 to 6
- row_weights: float32 [256, 2560], replicated
- memory_weights: float32 [256, 512], replicated, may hold values from -0.375 to 0.375
- down_weight: float32 [1024, 256], replicated, may hold values from -0.1875 to 0.1875
- vectors: float32 [11, 256], replicated
- row_momentum: float32 [256, 2560], replicated, may hold values from -0.25 to 0.25
- memory_momentum: float32 [256, 512], replicated, may hold values from -0.25 to 0.25
- down_momentum: float32 [1024, 256], replicated, may hold values from -0.25 to 0.25
- vector_momentum: float32 [11, 256], replicated, may hold values from -0.25 to 0.25
- row_average: float32 [256, 2560], replicated
- memory_average: float32 [256, 512], replicated, may hold values from -0.375 to 0.375
- down_average: float32 [1024, 256], replicated, may hold values from -0.1875 to 0.1875
- vector_average: float32 [11, 256], replicated
Outputs:
- output: float32 [4096, 256], P('dp')
- grad_actions: float32 [4096, 256], P('dp')
- grad_memory: float32 [256, 800, 256], P('dp', 'cond')
- row_momentum_new: float32 [256, 2560], replicated
- row_weights_new: float32 [256, 2560], replicated
- row_average_new: float32 [256, 2560], replicated
- memory_momentum_new: float32 [256, 512], replicated
- memory_weights_new: float32 [256, 512], replicated
- memory_average_new: float32 [256, 512], replicated
- down_momentum_new: float32 [1024, 256], replicated
- down_weight_new: float32 [1024, 256], replicated
- down_average_new: float32 [1024, 256], replicated
- vector_momentum_new: float32 [11, 256], replicated
- vectors_new: float32 [11, 256], replicated
- vector_average_new: float32 [11, 256], replicated
Inputs may be any that keep to these rules, and one draw needn't show every extreme that they name: `patch_flags`: every entry is 49 or 196.
All inputs are finite; a program needn't handle non-finite values. No bound on the sum of `memory_mask` on one device may be relied on, other than what follows from the above.
Results may differ from a plain program's by a relative error of at most 0.02.
Values may be sent and summed in bfloat16 or wider, within the bound.
A program may use at most 128 MiB of HBM per device.

v0:
```python
import functools
import math

import jax
import jax.numpy as jnp
from jax import lax
from jax.experimental import pallas as pl
from jax.experimental.pallas import tpu as pltpu
from jax.sharding import PartitionSpec as P

HEADS = 4
H = 16
PATCHES = 196
STEP = 10
INERTIA = 0.9
STEP_RATE = 1.0
LOWEST = -1e30
NB = 2
MESH = pl.DeviceIdType.MESH
MIB = 2**20
BF = jnp.bfloat16
F32 = jnp.float32


def half(values):
    return values.astype(BF)


def wide(values):
    return values.astype(F32)


def nn(a, b):
    return jnp.dot(a, b, preferred_element_type=F32)


def nt(a, b):
    return lax.dot_general(a, b, (((1,), (1,)), ((), ())), preferred_element_type=F32)


def tn(a, b):
    return lax.dot_general(a, b, (((0,), (0,)), ((), ())), preferred_element_type=F32)


def unit_rows(values):
    centered = values - jnp.mean(values, axis=-1, keepdims=True)
    rate = lax.rsqrt(jnp.mean(centered * centered, axis=-1, keepdims=True) + 1e-05)
    return centered * rate, rate


def unit_back(grad, unit, rate):
    return rate * (
        grad
        - jnp.mean(grad, axis=-1, keepdims=True)
        - unit * jnp.mean(grad * unit, axis=-1, keepdims=True)
    )


def column_sum(values):
    return jnp.sum(values, axis=0, keepdims=True)


def head_columns(table, first):
    rows = table.shape[0]
    low_lane = lax.broadcasted_iota(jnp.int32, (rows, 128), 1) < 64
    cols = [table[:, first + h : first + h + 1] for h in range(HEADS)]
    return jnp.concatenate(
        [jnp.where(low_lane, cols[0], cols[1]), jnp.where(low_lane, cols[2], cols[3])], axis=1
    )


def head_reduce(values, kind):
    rows = values.shape[0]
    low_lane = lax.broadcasted_iota(jnp.int32, (rows, 128), 1) < 64
    fill = LOWEST if kind == "max" else 0.0
    cols = []
    for pair in range(2):
        part = values[:, pair * 128 : pair * 128 + 128]
        for keep_low in (True, False):
            picked = jnp.where(low_lane == keep_low, part, fill)
            if kind == "max":
                cols.append(jnp.max(picked, axis=1, keepdims=True))
            else:
                cols.append(jnp.sum(picked, axis=1, keepdims=True))
    return cols


def spread(cols):
    rows = cols[0].shape[0]
    low_lane = lax.broadcasted_iota(jnp.int32, (rows, 128), 1) < 64
    return jnp.concatenate(
        [jnp.where(low_lane, cols[0], cols[1]), jnp.where(low_lane, cols[2], cols[3])], axis=1
    )


def lanes_of(cols):
    rows = cols[0].shape[0]
    lane = lax.broadcasted_iota(jnp.int32, (rows, 128), 1)
    table = jnp.zeros((rows, 128), F32)
    for h, col in enumerate(cols):
        table = jnp.where(lane == h, col, table)
    return table


def pad_rows(values, rows):
    missing = rows - values.shape[0]
    if missing == 0:
        return values
    return jnp.concatenate([values, jnp.zeros((missing, values.shape[1]), values.dtype)], axis=0)


def self_weights(q, k, blocks, causal):
    k_blocks = jnp.concatenate([k] * HEADS, axis=0) * blocks
    scores = jnp.where(causal, nt(q, k_blocks) * 0.125, LOWEST)
    top = spread(head_reduce(scores, "max"))
    raised = jnp.where(causal, jnp.exp(scores - top), 0.0)
    total = spread(head_reduce(raised, "sum"))
    return raised / total, k_blocks


class Names:
    pass


def layer_kernel(names, sizes, *refs):
    r = Names()
    for name, ref in zip(names, refs, strict=True):
        setattr(r, name, ref)
    rows, samples, slots, n_cond, n_dp, width = sizes
    hidden = r.dw.shape[0]
    part_rows = rows // NB
    own = part_rows // n_cond
    part_samples = samples // NB
    c = lax.axis_index("cond")
    d = lax.axis_index("dp")

    def peer(k):
        return (d, lax.rem(c + k, n_cond))

    core_peer = (d, c + 1 - 2 * lax.rem(c, 2))
    chip_peer = (d, lax.rem(c + 2, n_cond))
    bit0 = lax.rem(c, 2)
    bit1 = c // 2

    def row(k):
        return (lax.rem(d + k, n_dp), c)

    barrier = pltpu.get_barrier_semaphore()
    for k in range(1, n_cond):
        pl.semaphore_signal(barrier, inc=1, device_id=peer(k), device_id_type=MESH)
    for k in range(1, n_dp):
        pl.semaphore_signal(barrier, inc=1, device_id=row(k), device_id_type=MESH)

    loads = {}

    def load(name, src, dst, at):
        copy = pltpu.make_async_copy(src, dst, r.load_sem.at[at])
        copy.start()
        loads[name] = copy

    load("act", r.act_h, r.act, 0)
    load("rw", r.rw_h, r.rw, 1)
    load("vec", r.vec_h, r.vec, 2)
    load("mw", r.mw_h, r.mw, 3)
    mem_parts = 4
    mem_rows = samples * slots // mem_parts
    for i in range(mem_parts):
        span = pl.ds(i * mem_rows, mem_rows)
        load(f"mem{i}", r.mem_h.at[span], r.mem.at[span], 8 + i)
    load("mask", r.mask_h, r.mask, 4)
    load("flag", r.flag_h, r.flag, 5)
    load("dw", r.dw_h, r.dw, 6)
    load("cot", r.cot_h, r.cot, 7)

    lane256 = lax.broadcasted_iota(jnp.int32, (256, 256), 1)
    row256 = lax.broadcasted_iota(jnp.int32, (256, 256), 0)
    r.blocks[...] = half(jnp.where(lane256 // 64 == row256 // 64, 1.0, 0.0))
    lane64 = lax.broadcasted_iota(jnp.int32, (64, 256), 1)
    row64 = lax.broadcasted_iota(jnp.int32, (64, 256), 0)
    r.heads[...] = jnp.where(lane64 // 64 == row64 // 16, 1.0, 0.0)
    r.heads_b[...] = half(r.heads[...])

    def causal_mask():
        key = lax.rem(lane64, 64)
        return (key // H == row64 // H) & (key <= row64)

    loads["act"].wait()
    loads["rw"].wait()
    loads["vec"].wait()

    @pl.loop(0, 4)
    def _(i):
        span = pl.ds(pl.multiple_of(i * 64, 64), 64)
        r.rwb[span, :] = half(r.rw[span, :])

    def vec(i):
        return r.vec[i : i + 1, :]

    w_qkv = lambda: r.rwb[:, : 3 * width]
    w_so = lambda: r.rwb[:, 3 * width : 4 * width]
    w_cq = lambda: r.rwb[:, 4 * width : 5 * width]
    w_co = lambda: r.rwb[:, 5 * width : 6 * width]
    w_up = lambda: r.rwb[:, 6 * width :]

    def self_forward(b):
        group = 128

        @pl.loop(0, part_rows // group)
        def _(g):
            span = pl.ds(pl.multiple_of(b * part_rows + g * group, group), group)
            x = r.act[span, :]
            unit, _ = unit_rows(x)
            a1 = half(unit * vec(0) + vec(1))
            r.a1[span, :] = a1
            qkv = half(nn(a1, w_qkv()))
            r.qkv[span, :] = qkv
            causal = causal_mask()
            blocks = r.blocks[...]
            mixed = []
            for s in range(group // 64):
                piece = qkv[s * 64 : s * 64 + 64, :]
                q, k, v = (piece[:, i * width : (i + 1) * width] for i in range(3))
                weights, _ = self_weights(q, k, blocks, causal)
                v_blocks = jnp.concatenate([v] * HEADS, axis=0) * blocks
                mixed.append(nn(half(weights), v_blocks))
            o1 = half(jnp.concatenate(mixed, axis=0))
            r.o1[span, :] = o1
            x1 = x + nn(o1, w_so())
            r.x1[span, :] = x1
            unit2, _ = unit_rows(x1)
            a2 = half(unit2 * vec(2) + vec(3))
            r.a2[span, :] = a2
            r.qs[span, :] = half(nn(a2, w_cq()) * 0.125)

    def pair_forward(b):
        batch = 4
        step = batch * slots

        @pl.loop(0, part_samples // batch)
        def _(g):
            first = b * part_samples + g * batch
            span = pl.ds(pl.multiple_of(first * slots, step), step)
            chunk = r.mem[span, :]
            for side in range(2):
                cols = slice(side * width, (side + 1) * width)
                kv = nn(chunk, r.mwb[:, cols])
                for s in range(batch):
                    r.kv[first + s, :, cols] = half(kv[s * slots : (s + 1) * slots, :])

    def usable_rows():
        position = lax.broadcasted_iota(jnp.int32, (samples, slots), 1)
        kept = (position < r.flag[...]) & (r.mask[...] == 1)
        time_token = (position == PATCHES) & (c == 0)
        r.use[...] = jnp.where(kept | time_token, 1.0, 0.0)

    def cross_forward(b):
        unroll = 2

        @pl.loop(0, part_samples // unroll)
        def _(g):
            for i in range(unroll):
                s = b * part_samples + g * unroll + i
                span = pl.ds(pl.multiple_of(s * H, H), H)
                q = jnp.concatenate([r.qs[span, :]] * HEADS, axis=0) * r.heads_b[...]
                usable = jnp.broadcast_to(r.use[pl.ds(s, 1), :], (64, slots)) > 0.5
                scores = jnp.where(usable, nt(q, r.kv[s, :, :width]), LOWEST)
                top = jnp.max(scores, axis=1, keepdims=True)
                raised = jnp.where(usable, jnp.exp(scores - top), 0.0)
                total = jnp.sum(raised, axis=1, keepdims=True)
                p = half(raised)
                r.p[s] = p
                mixed = nn(p, r.kv[s, :, width:]) * r.heads[...]
                r.o_out[span, :] = half(sum(mixed[h * H : h * H + H, :] for h in range(HEADS)))
                r.top[span, :] = lanes_of([top[h * H : h * H + H, :] for h in range(HEADS)])
                r.total[span, :] = lanes_of([total[h * H : h * H + H, :] for h in range(HEADS)])

    pending = []

    def send(src, dst, at, to):
        copy = pltpu.make_async_remote_copy(
            src_ref=src,
            dst_ref=dst,
            send_sem=r.ssem.at[at],
            recv_sem=r.rsem.at[at],
            device_id=to,
            device_id_type=MESH,
        )
        copy.start()
        pending.append(copy)
        return copy

    def own_span(b, owner):
        return pl.ds(pl.multiple_of(b * part_rows + owner * own, own), own)

    flights = {}

    def send_mixed(b):
        for k in range(n_cond):
            owner = lax.rem(c + k, n_cond)
            span = own_span(b, owner)
            stats = jnp.concatenate(
                [
                    pad_rows(r.top[span, :], 128).T[:8, :],
                    pad_rows(r.total[span, :], 128).T[:8, :],
                ],
                axis=0,
            )
            if k == 0:
                r.st_in[b, 0] = stats
                r.o_in[b, 0] = r.o_out[span, :]
            else:
                r.st_out[b, k] = stats
                at = (b * n_cond + k) * 2
                flights["o", b, k] = (
                    send(r.st_out.at[b, k], r.st_in.at[b, k], at, peer(k)),
                    send(r.o_out.at[span, :], r.o_in.at[b, k], at + 1, peer(k)),
                )

    def middle(b):
        for k in range(1, n_cond):
            for copy in flights["o", b, k]:
                copy.wait_recv()
        me = own_span(b, c)
        mine = pl.ds(b * own, own)
        tops = [r.st_in[b, k, :8, :] for k in range(n_cond)]
        top = functools.reduce(jnp.maximum, tops)
        raised = [jnp.exp(t - top) for t in tops]
        total = sum(w * r.st_in[b, k, 8:, :] for k, w in enumerate(raised))
        total = jnp.maximum(total, 0.5)
        shares = [w / total for w in raised]
        table = pad_rows(jnp.concatenate(shares, axis=0), 128).T[:own, :]
        spreads = [head_columns(table, 8 * k) for k in range(n_cond)]
        o2 = sum(spreads[k] * wide(r.o_in[b, k]) for k in range(n_cond))
        o2b = half(o2)
        r.o2[mine, :] = o2b
        x2 = r.x1[me, :] + nn(o2b, w_co())
        unit, rate = unit_rows(x2)
        a3 = half(unit * vec(4) + vec(5))
        r.a3[mine, :] = a3
        biases = hidden // width
        cot = r.cot[me, :]
        dz = half(cot)
        r.dz[mine, :] = dz
        out = x2 + vec(6 + biases)
        da3 = jnp.zeros((own, width), F32)
        for j in range(biases):
            cols = slice(6 * width + j * width, 6 * width + (j + 1) * width)
            here = slice(j * width, (j + 1) * width)
            u = nn(a3, r.rwb[:, cols]) + vec(6 + j)
            below = 0.5 + 0.5 * lax.erf(u * (2.0**-0.5))
            hb = half(u * below)
            r.hb[mine, here] = hb
            out = out + nn(hb, r.dwb[here, :])
            slope = below + u * (jnp.exp(-0.5 * u * u) * (1.0 / math.sqrt(2.0 * math.pi)))
            du = half(nt(dz, r.dwb[here, :]) * slope)
            r.du[mine, here] = du
            add_vec(b, 6 + j, column_sum(wide(du)))
            da3 = da3 + nt(du, r.rwb[:, cols])
        r.out16[me, :] = half(out)
        add_vec(b, 6 + biases, column_sum(wide(dz)))
        add_vec(b, 4, column_sum(da3 * unit))
        add_vec(b, 5, column_sum(da3))
        dx2 = cot + unit_back(da3 * vec(4), unit, rate)
        r.dx2[mine, :] = dx2
        dy = half(dx2)
        r.dy2[mine, :] = dy
        do2 = wide(half(nt(dy, w_co())))
        delta = lanes_of(head_reduce(do2 * wide(o2b), "sum"))
        delta = pad_rows(delta, 128).T[:8, :]
        for k in range(n_cond):
            grads = half(do2 * spreads[k])
            dots = delta * shares[k]
            if k == 0:
                r.do_in[me, :] = grads
                r.dl_in[b, 0] = dots
            else:
                r.do_out[b, k] = grads
                r.dl_out[b, k] = dots
                at = (NB * n_cond + b * n_cond + k) * 2
                to = peer(n_cond - k)
                flights["do", b, k] = (
                    send(r.dl_out.at[b, k], r.dl_in.at[b, k], at, to),
                    send(r.do_out.at[b, k], r.do_in.at[me, :], at + 1, to),
                )

    def add_vec(b, i, values):
        if b == 0:
            r.vg[i : i + 1, :] = values
        else:
            r.vg[i : i + 1, :] += values

    def cross_backward(b):
        for k in range(n_cond):
            owner = lax.rem(c + k, n_cond)
            if k:
                for copy in flights["do", b, k]:
                    copy.wait_recv()
            r.dl[own_span(b, owner), :] = pad_rows(r.dl_in[b, k], 128).T[:own, :]
        unroll = 2

        @pl.loop(0, part_samples // unroll)
        def _(g):
            pairs = []
            first = b * part_samples + g * unroll
            for i in range(unroll):
                s = first + i
                span = pl.ds(pl.multiple_of(s * H, H), H)
                heads_b = r.heads_b[...]
                q = jnp.concatenate([r.qs[span, :]] * HEADS, axis=0) * heads_b
                grads = jnp.concatenate([r.do_in[span, :]] * HEADS, axis=0) * heads_b
                dots = r.dl[span, :]
                dots = jnp.concatenate([dots[:, h : h + 1] for h in range(HEADS)], axis=0)
                p = r.p[s]
                ds = half(wide(p) * (nt(grads, r.kv[s, :, width:]) - dots))
                dq = nn(ds, r.kv[s, :, :width]) * r.heads[...]
                dq = sum(dq[h * H : h * H + H, :] for h in range(HEADS)) * 0.125
                r.dq_out[span, :] = half(dq)
                pairs.append(jnp.concatenate([tn(ds, q), tn(p, grads)], axis=1))
            span = pl.ds(pl.multiple_of(first * slots, unroll * slots), unroll * slots)
            r.dkv[span, :] = half(jnp.concatenate(pairs, axis=0))

    def send_query_grads(b):
        for k in range(1, n_cond):
            owner = lax.rem(c + k, n_cond)
            at = 4 * NB * n_cond + b * n_cond + k
            flights["dq", b, k] = send(
                r.dq_out.at[own_span(b, owner), :], r.dq_in.at[b, k], at, peer(k)
            )

    def self_backward(b):
        me = own_span(b, c)
        mine = pl.ds(b * own, own)
        total = wide(r.dq_out[me, :])
        for k in range(1, n_cond):
            flights["dq", b, k].wait_recv()
            total = total + wide(r.dq_in[b, k])
        dqc = half(total)
        r.dqc[mine, :] = dqc
        da2 = nt(dqc, w_cq())
        unit2, rate2 = unit_rows(r.x1[me, :])
        add_vec(b, 2, column_sum(da2 * unit2))
        add_vec(b, 3, column_sum(da2))
        dx1 = r.dx2[mine, :] + unit_back(da2 * vec(2), unit2, rate2)
        dy1 = half(dx1)
        r.dy1[mine, :] = dy1
        do1 = half(nt(dy1, w_so()))
        causal = causal_mask()
        blocks = r.blocks[...]
        pieces = []
        for s in range(own // 64):
            span = pl.ds(pl.multiple_of(b * part_rows + c * own + s * 64, 64), 64)
            q, k, v = (r.qkv[span, i * width : (i + 1) * width] for i in range(3))
            grads = do1[s * 64 : s * 64 + 64, :]
            weights, k_blocks = self_weights(q, k, blocks, causal)
            v_blocks = jnp.concatenate([v] * HEADS, axis=0) * blocks
            dv = tn(half(weights), grads) * wide(blocks)
            dp = nt(grads, v_blocks)
            dots = spread(head_reduce(weights * dp, "sum"))
            ds = half(weights * (dp - dots))
            dq = nn(ds, k_blocks) * 0.125
            dk = tn(ds, q) * wide(blocks)
            dk = sum(dk[h * 64 : h * 64 + 64, :] for h in range(HEADS)) * 0.125
            dv = sum(dv[h * 64 : h * 64 + 64, :] for h in range(HEADS))
            pieces.append(half(jnp.concatenate([dq, dk, dv], axis=1)))
        dqkv = jnp.concatenate(pieces, axis=0)
        r.dqkv[mine, :] = dqkv
        da1 = nt(dqkv, w_qkv())
        unit1, rate1 = unit_rows(r.act[me, :])
        add_vec(b, 0, column_sum(da1 * unit1))
        add_vec(b, 1, column_sum(da1))
        r.ga16[me, :] = half(dx1 + unit_back(da1 * vec(0), unit1, rate1))

    layout = {"ffn": (0, 2 * hidden), "row": (2 * hidden, 6 * width)}
    layout["pair"] = (2 * hidden + 6 * width, 2 * width)
    set_at = {name: 5 * NB * n_cond + 8 + 6 * i for i, name in enumerate(layout)}

    def owned(ref, dyn):
        return jnp.concatenate([ref[own_span(b, c), :] for b in range(NB)], axis=0)

    def ffn_grads():
        for j in range(hidden // width):
            here = slice(j * width, (j + 1) * width)
            r.g[j * width : (j + 1) * width, :] = half(tn(r.a3[...], r.du[:, here]))
            at = hidden + j * width
            r.g[at : at + width, :] = half(tn(r.hb[:, here], r.dz[...]))

    def put_row(j, values):
        first = layout["row"][0] + j * width
        r.g[first : first + width, :] = half(values)

    def row_grads():
        put_row(0, tn(r.o2[...], r.dy2[...]))
        put_row(1, tn(owned(r.a2, c), r.dqc[...]))
        put_row(2, tn(owned(r.o1, c), r.dy1[...]))
        a1 = owned(r.a1, c)
        for j in range(3):
            put_row(3 + j, tn(a1, r.dqkv[:, j * width : (j + 1) * width]))

    def pair_grads():
        step = 2 * slots
        r.gw[...] = jnp.zeros_like(r.gw)

        @pl.loop(0, samples // 2)
        def _(g):
            span = pl.ds(pl.multiple_of(g * step, step), step)
            r.gw[...] += tn(r.mem[span, :], r.dkv[span, :])

        first = layout["pair"][0]
        for side in range(2):
            r.g[first + side * width : first + (side + 1) * width, :] = half(
                r.gw[:, side * width : (side + 1) * width]
            )

    def set_sizes(name):
        first, count = layout[name]
        quarter = count // 4
        piece = max(16, quarter // n_dp)
        return first, count, count // 2, quarter, piece, quarter // piece

    def at_rows(start, count):
        return pl.ds(pl.multiple_of(start, 16), count)

    def reduce_core(name):
        first, count, two, four, piece, owners = set_sizes(name)
        flights[name, 0] = send(
            r.g.at[at_rows(first + (1 - bit0) * two, two), :],
            r.rc.at[at_rows(first // 2, two), :],
            set_at[name],
            core_peer,
        )

    def reduce_chip(name):
        first, count, two, four, piece, owners = set_sizes(name)
        flights[name, 0].wait_recv()
        base = first // 2
        for q in range(2):
            span = pl.ds(base + q * four, four)
            got = wide(r.rc[span, :]) + wide(
                r.g[at_rows(first + bit0 * two + q * four, four), :]
            )
            r.rc[span, :] = half(got)
        flights[name, 1] = send(
            r.rc.at[at_rows(base + (1 - bit1) * four, four), :],
            r.ry.at[pl.ds(first // 4, four), :],
            set_at[name] + 1,
            chip_peer,
        )

    def wait_bytes(name, stage, ref, count, which):
        view = ref.at[pl.ds(0, count), :]
        copy = pltpu.make_async_remote_copy(
            src_ref=view,
            dst_ref=view,
            send_sem=r.ssem.at[set_at[name] + stage],
            recv_sem=r.rsem.at[set_at[name] + stage],
            device_id=core_peer,
            device_id_type=MESH,
        )
        if which == "recv":
            copy.wait_recv()
        else:
            copy.wait_send()

    def start(src, dst, at, to):
        pltpu.make_async_remote_copy(
            src_ref=src,
            dst_ref=dst,
            send_sem=r.ssem.at[at],
            recv_sem=r.rsem.at[at],
            device_id=to,
            device_id_type=MESH,
        ).start()

    def guard(full, cond, body):
        if full:
            body()
        else:
            pl.when(cond)(body)

    def reduce_rows(name):
        first, count, two, four, piece, owners = set_sizes(name)
        flights[name, 1].wait_recv()
        base = first // 4
        mine = wide(r.rc[at_rows(first // 2 + bit1 * four, four), :])
        span = pl.ds(base, four)
        r.ry[span, :] = half(mine + wide(r.ry[span, :]))
        for k in range(1, n_dp):
            to = lax.rem(d + k, n_dp)

            def go(k=k, to=to):
                start(
                    r.ry.at[at_rows(base + to * piece, piece), :],
                    r_rd(name).at[pl.ds(k * piece, piece), :],
                    set_at[name] + 2,
                    row(k),
                )

            guard(owners == n_dp, to < owners, go)

    def r_rd(name):
        return getattr(r, "rd_" + name)

    def quarter_at(name):
        first, count, two, four, piece, owners = set_sizes(name)
        return first + bit0 * two + bit1 * four

    def gather_rows(name):
        first, count, two, four, piece, owners = set_sizes(name)
        base = first // 4

        def finish():
            wait_bytes(name, 2, r_rd(name), (n_dp - 1) * piece, "recv")
            total = wide(r.ry[at_rows(base + d * piece, piece), :])
            for k in range(1, n_dp):
                total = total + wide(r_rd(name)[k * piece : (k + 1) * piece, :])
            here = at_rows(quarter_at(name) + d * piece, piece)
            r.tot[here, :] = half(total)
            for k in range(1, n_dp):
                start(r.tot.at[here, :], r.tot.at[here, :], set_at[name] + 3, row(k))

        guard(owners == n_dp, d < owners, finish)

    def gather_chip(name):
        first, count, two, four, piece, owners = set_sizes(name)
        if owners == n_dp:
            wait_bytes(name, 3, r.tot, (n_dp - 1) * piece, "recv")
        else:
            pl.when(d < owners)(
                lambda: wait_bytes(name, 3, r.tot, (owners - 1) * piece, "recv")
            )
            pl.when(d >= owners)(lambda: wait_bytes(name, 3, r.tot, owners * piece, "recv"))
        span = at_rows(quarter_at(name), four)
        flights[name, 4] = send(
            r.tot.at[span, :], r.tot.at[span, :], set_at[name] + 4, chip_peer
        )

    def gather_core(name):
        first, count, two, four, piece, owners = set_sizes(name)
        flights[name, 4].wait_recv()
        span = at_rows(first + bit0 * two, two)
        flights[name, 5] = send(
            r.tot.at[span, :], r.tot.at[span, :], set_at[name] + 5, core_peer
        )

    def end_set(name):
        first, count, two, four, piece, owners = set_sizes(name)
        flights[name, 5].wait_recv()
        if owners == n_dp:
            wait_bytes(name, 2, r.ry, (n_dp - 1) * piece, "send")
            wait_bytes(name, 3, r.tot, (n_dp - 1) * piece, "send")
        else:
            pl.when(d < owners)(
                lambda: wait_bytes(name, 2, r.ry, (owners - 1) * piece, "send")
            )
            pl.when(d >= owners)(lambda: wait_bytes(name, 2, r.ry, owners * piece, "send"))
            pl.when(d < owners)(lambda: wait_bytes(name, 3, r.tot, (n_dp - 1) * piece, "send"))

    vec_at = 5 * NB * n_cond + 8 + 6 * len(layout)

    def small_cond():
        r.vc_in[pl.ds(c, 1)] = r.vg[...][None]
        for k in range(1, n_cond):
            flights["vc", k] = send(r.vg, r.vc_in.at[c], vec_at + k - 1, peer(k))

    def small_rows():
        for k in range(1, n_cond):
            flights["vc", k].wait_recv()
        r.vd_in[pl.ds(d, 1)] = sum(r.vc_in[k] for k in range(n_cond))[None]
        for k in range(1, n_dp):
            start(r.vd_in.at[d], r.vd_in.at[d], vec_at + 3, row(k))

    def small_wait(which):
        view = r.vd_in.at[pl.ds(0, n_dp - 1)]
        copy = pltpu.make_async_remote_copy(
            src_ref=view,
            dst_ref=view,
            send_sem=r.ssem.at[vec_at + 3],
            recv_sem=r.rsem.at[vec_at + 3],
            device_id=core_peer,
            device_id_type=MESH,
        )
        copy.wait_recv() if which == "recv" else copy.wait_send()

    def small_end():
        small_wait("recv")
        total = r.vd_in[0]
        for k in range(1, n_dp):
            total = total + r.vd_in[k]
        r.vtot[...] = total
        small_wait("send")

    def share(name, ref, b):
        span = own_span(b, c)
        for k in range(1, n_cond):
            flights[name, b, k] = send(
                ref.at[span, :], ref.at[span, :], vec_at + 4 + len(shared), peer(k)
            )
            shared.append((name, b, k))

    shared = []

    r.vg[11:16, :] = jnp.zeros((5, width), F32)
    self_forward(0)
    loads["mw"].wait()
    r.mwb[...] = half(r.mw[...])
    loads["mask"].wait()
    loads["flag"].wait()
    usable_rows()
    for i in range(mem_parts // NB):
        loads[f"mem{i}"].wait()
    pair_forward(0)
    cross_forward(0)
    pl.semaphore_wait(barrier, n_cond - 1 + n_dp - 1)
    send_mixed(0)
    loads["dw"].wait()
    r.dwb[...] = half(r.dw[...])
    loads["cot"].wait()
    for b in range(1, NB):
        self_forward(b)
        for i in range(b * mem_parts // NB, (b + 1) * mem_parts // NB):
            loads[f"mem{i}"].wait()
        pair_forward(b)
        cross_forward(b)
        send_mixed(b)
    for b in range(NB):
        middle(b)
    ffn_grads()
    reduce_core("ffn")
    for b in range(NB):
        cross_backward(b)
        send_query_grads(b)
        if b == 0:
            reduce_chip("ffn")
        if b == NB - 1:
            reduce_rows("ffn")
    pair_grads()
    reduce_core("pair")
    for b in range(NB):
        self_backward(b)
        if b == 0:
            reduce_chip("pair")
            gather_rows("ffn")
    small_cond()
    row_grads()
    reduce_core("row")
    reduce_rows("pair")
    gather_chip("ffn")
    reduce_chip("row")
    small_rows()
    gather_rows("pair")
    reduce_rows("row")
    for b in range(NB):
        share("out16", r.out16, b)
        share("ga16", r.ga16, b)
    gather_core("ffn")
    gather_chip("pair")
    gather_rows("row")
    gather_core("pair")
    gather_chip("row")
    gather_core("row")
    small_end()
    for key in shared:
        flights[key].wait_recv()
    for name in layout:
        end_set(name)
    for copy in pending:
        copy.wait_send()


def step_kernel(names, token_count, *refs):
    r = Names()
    for name, ref in zip(names, refs, strict=True):
        setattr(r, name, ref)
    width = r.w_p.shape[0]
    hidden = r.w_d.shape[0]
    keep = 1.0 - (1.0 + STEP) ** (-0.75)
    copies = []

    def store(src, dst):
        copy = pltpu.make_async_copy(src, dst, r.sem.at[len(copies)])
        copy.start()
        copies.append(copy)

    r.mwb[...] = half(r.w_p[...])
    total_rows = r.dkv.shape[0]
    chunks = 8
    step = total_rows // chunks
    for i in range(chunks):
        inner = 2
        small = step // inner

        @pl.loop(0, inner)
        def _(j, i=i):
            span = pl.ds(pl.multiple_of(i * step + j * small, 16), small)
            r.gm[span, :] = nt(r.dkv[span, :], r.mwb[...])

        span = pl.ds(i * step, step)
        store(r.gm.at[span, :], r.gm_h.at[span, :])
    r.out[...] = wide(r.out16[...])
    store(r.out, r.out_h)
    r.ga[...] = wide(r.ga16[...])
    store(r.ga, r.ga_h)

    def update(weight, grad, moment, average):
        scaled = grad / token_count
        moment_new = INERTIA * moment + scaled
        weight_new = weight - STEP_RATE * (scaled + INERTIA * moment_new)
        average_new = keep * average + (1.0 - keep) * weight_new
        return moment_new, weight_new, average_new

    def group(prefix, views):
        w, m, a = (getattr(r, kind + "_" + prefix) for kind in "wma")
        for rows, cols, grad in views:
            new = update(w[rows, cols], grad(), m[rows, cols], a[rows, cols])
            for kind, value in zip("mwa", new):
                getattr(r, prefix + kind)[rows, cols] = value
        for kind in "mwa":
            store(getattr(r, prefix + kind), getattr(r, prefix + kind + "_h"))

    every = slice(None)
    row_first = 2 * hidden
    pair_first = row_first + 6 * width
    order = {5: 0, 4: 1, 3: 2, 0: 3, 1: 4, 2: 5}

    def table(first):
        return lambda: wide(r.tot[first : first + width, :])

    group(
        "d",
        [
            (slice(j * width, (j + 1) * width), every, table(hidden + j * width))
            for j in range(hidden // width)
        ],
    )
    group(
        "r",
        [
            (every, slice(j * width, (j + 1) * width), table(row_first + order[j] * width))
            for j in range(6)
        ]
        + [
            (every, slice((6 + j) * width, (7 + j) * width), table(j * width))
            for j in range(hidden // width)
        ],
    )
    group(
        "p",
        [
            (every, slice(j * width, (j + 1) * width), table(pair_first + j * width))
            for j in range(2)
        ],
    )
    group("v", [(every, every, lambda: r.vtot[: r.w_v.shape[0], :])])
    for copy in copies:
        copy.wait()


def per_device(
    actions,
    memory,
    patch_flags,
    memory_mask,
    cotangent,
    row_weights,
    memory_weights,
    down_weight,
    vectors,
    row_momentum,
    memory_momentum,
    down_momentum,
    vector_momentum,
    row_average,
    memory_average,
    down_average,
    vector_average,
):
    rows, width = actions.shape
    samples = rows // H
    slots = memory.shape[1]
    hidden = down_weight.shape[0]
    n_cond = lax.axis_size("cond")
    n_dp = lax.axis_size("dp")
    part_rows = rows // NB
    own = part_rows // n_cond
    total = 2 * hidden + 8 * width
    flat = samples * slots
    ins = {
        "act_h": actions,
        "mem_h": memory.reshape(flat, width),
        "mask_h": memory_mask,
        "flag_h": patch_flags,
        "cot_h": cotangent,
        "rw_h": row_weights,
        "mw_h": memory_weights,
        "dw_h": down_weight,
        "vec_h": vectors,
    }
    outs = {
        "tot": ((total, width), BF),
        "vtot": ((16, width), F32),
        "dkv": ((flat, 2 * width), BF),
        "out16": ((rows, width), BF),
        "ga16": ((rows, width), BF),
    }

    def pieces(count):
        return n_dp * max(16, count // 4 // n_dp)

    scratch = {
        "act": ((rows, width), F32),
        "rw": (row_weights.shape, F32),
        "vec": (vectors.shape, F32),
        "mw": (memory_weights.shape, F32),
        "mem": ((flat, width), BF),
        "mask": (memory_mask.shape, jnp.int32),
        "flag": (patch_flags.shape, jnp.int32),
        "dw": (down_weight.shape, F32),
        "cot": ((rows, width), F32),
        "rwb": (row_weights.shape, BF),
        "mwb": (memory_weights.shape, BF),
        "dwb": (down_weight.shape, BF),
        "blocks": ((256, 256), BF),
        "heads": ((64, 256), F32),
        "heads_b": ((64, 256), BF),
        "a1": ((rows, width), BF),
        "qkv": ((rows, 3 * width), BF),
        "o1": ((rows, width), BF),
        "x1": ((rows, width), F32),
        "a2": ((rows, width), BF),
        "qs": ((rows, width), BF),
        "kv": ((samples, slots, 2 * width), BF),
        "use": ((samples, slots), F32),
        "p": ((samples, 64, slots), BF),
        "o_out": ((rows, width), BF),
        "top": ((rows, 128), F32),
        "total": ((rows, 128), F32),
        "st_in": ((NB, n_cond, 16, 128), F32),
        "st_out": ((NB, n_cond, 16, 128), F32),
        "o_in": ((NB, n_cond, own, width), BF),
        "o2": ((NB * own, width), BF),
        "a3": ((NB * own, width), BF),
        "dz": ((NB * own, width), BF),
        "hb": ((NB * own, hidden), BF),
        "du": ((NB * own, hidden), BF),
        "dx2": ((NB * own, width), F32),
        "dy2": ((NB * own, width), BF),
        "dqc": ((NB * own, width), BF),
        "dy1": ((NB * own, width), BF),
        "dqkv": ((NB * own, 3 * width), BF),
        "do_in": ((rows, width), BF),
        "do_out": ((NB, n_cond, own, width), BF),
        "dl_in": ((NB, n_cond, 8, 128), F32),
        "dl_out": ((NB, n_cond, 8, 128), F32),
        "dl": ((rows, 128), F32),
        "dq_out": ((rows, width), BF),
        "dq_in": ((NB, n_cond, own, width), BF),
        "vg": ((16, width), F32),
        "vc_in": ((n_cond, 16, width), F32),
        "vd_in": ((n_dp, 16, width), F32),
        "g": ((total, width), BF),
        "gw": ((width, 2 * width), F32),
        "rc": ((total // 2, width), BF),
        "ry": ((total // 4, width), BF),
        "rd_ffn": ((pieces(2 * hidden), width), BF),
        "rd_row": ((pieces(6 * width), width), BF),
        "rd_pair": ((pieces(2 * width), width), BF),
    }
    sems = {
        "load_sem": pltpu.SemaphoreType.DMA((16,)),
        "ssem": pltpu.SemaphoreType.DMA((96,)),
        "rsem": pltpu.SemaphoreType.DMA((96,)),
    }
    whole = pl.BlockSpec(memory_space=pltpu.VMEM)
    far = pl.BlockSpec(memory_space=pl.ANY)
    names = list(ins) + list(outs) + list(scratch) + list(sems)
    sizes = (rows, samples, slots, n_cond, n_dp, width)
    tot, vtot, dkv, out16, ga16 = pl.pallas_call(
        functools.partial(layer_kernel, names, sizes),
        out_shape=[jax.ShapeDtypeStruct(*v) for v in outs.values()],
        in_specs=[far] * len(ins),
        out_specs=[whole] * len(outs),
        scratch_shapes=[pltpu.VMEM(*v) for v in scratch.values()] + list(sems.values()),
        compiler_params=pltpu.CompilerParams(
            collective_id=0, has_side_effects=True, vmem_limit_bytes=44 * MIB
        ),
        name="layer",
    )(*ins.values())

    ins2 = {
        "tot": tot,
        "vtot": vtot,
        "dkv": dkv,
        "out16": out16,
        "ga16": ga16,
        "w_r": row_weights,
        "w_p": memory_weights,
        "w_d": down_weight,
        "w_v": vectors,
        "m_r": row_momentum,
        "m_p": memory_momentum,
        "m_d": down_momentum,
        "m_v": vector_momentum,
        "a_r": row_average,
        "a_p": memory_average,
        "a_d": down_average,
        "a_v": vector_average,
    }
    outs2 = {
        "out": (rows, width),
        "ga": (rows, width),
        "gm": (flat, width),
    }
    for prefix, array in (("r", row_weights), ("p", memory_weights), ("d", down_weight), ("v", vectors)):
        for kind in "mwa":
            outs2[prefix + kind] = array.shape
    names2 = list(ins2) + [k + "_h" for k in outs2] + list(outs2) + ["mwb", "sem"]
    results = pl.pallas_call(
        functools.partial(step_kernel, names2, float(rows * n_dp)),
        out_shape=[jax.ShapeDtypeStruct(v, F32) for v in outs2.values()],
        in_specs=[whole] * len(ins2),
        out_specs=[far] * len(outs2),
        scratch_shapes=[pltpu.VMEM(v, F32) for v in outs2.values()]
        + [pltpu.VMEM(memory_weights.shape, BF), pltpu.SemaphoreType.DMA((32,))],
        compiler_params=pltpu.CompilerParams(vmem_limit_bytes=60 * MIB),
        name="step",
    )(*ins2.values())
    out, ga, gm = results[:3]
    return (out, ga, gm.reshape(samples, slots, width), *results[3:])


def solution(mesh):
    in_specs = (
        P("dp", None),
        P("dp", "cond", None),
        P("dp", "cond"),
        P("dp", "cond"),
        P("dp", None),
    ) + (P(),) * 12
    out_specs = (P("dp", None), P("dp", None), P("dp", "cond", None)) + (P(),) * 12
    return jax.shard_map(
        per_device, mesh=mesh, in_specs=in_specs, out_specs=out_specs, check_vma=False
    )
```

profile of v0, /device:TPU:1, one launch (start us, length us, event | category | flops | bytes accessed | tf_op | source)
XLA Modules:
  0.0 122.8 jit_solution(7833252584809148546)
XLA Ops:
  0.6 0.7 copy.32.refs_3_
  1.4 0.0 copy-start
  1.4 1.7 %copy-done = f32[256,2560]{1,0:T(8,128)S(1)} copy-done((f32[256,2560]{1,0:T(8,128)S(1)}, f32[256,2560]{1,0:T(8,128)}, u32[]{:S(2)}) %copy-start) | copy-done | bytes 2621464
  3.1 0.0 copy-start.1
  3.1 1.2 copy-done.1
  4.3 0.0 copy-start.2
  4.3 1.0 copy-done.2
  5.4 0.0 copy-start.4
  5.4 1.0 copy-done.4
  6.4 0.0 copy-start.5
  6.4 1.0 copy-done.5
  7.5 0.0 copy-start.8
  7.5 0.7 copy-done.8
  8.2 0.0 copy-start.9
  8.2 0.8 copy-done.9
  8.9 92.9 %layer.1 = (bf16[4096,256]{1,0:T(8,128)(2,1)S(1)}, f32[16,256]{1,0:T(8,128)S(1)}, bf16[6400,512]{1,0:T(8,128)(2,1)}, bf16[512,256]{1,0:T(8,128)(2,1)S(1)}, bf16[512,256]{1,0:T(8,128)(2,1)S(1)}) custom-call(f32[512,256]{1,0:T(8,128)S(1)} %copy-done.4, bf16[6400,256]{1,0:T(8,128)(2,1)} %bitcast.2, s32[32,200]{1,0:T(8,128)S(1)} %copy-done.9, ...), custom_call_target="tpu_custom_call" | custom-call | tf_op jit(solution)/shard_map/layer/pallas_call | solution.py:977
  101.9 0.0 copy-start.3
  101.9 1.4 %copy-done.3 = bf16[4096,256]{1,0:T(8,128)(2,1)} copy-done((bf16[4096,256]{1,0:T(8,128)(2,1)}, bf16[4096,256]{1,0:T(8,128)(2,1)S(1)}, u32[]{:S(2)}) %copy-start.3) | copy-done | bytes 2097176
  103.3 0.0 copy-start.6
  103.3 0.7 copy-done.6
  104.0 0.0 copy-start.7
  104.0 0.7 copy-done.7
  104.7 0.0 copy-start.10
  104.7 0.6 copy-done.10
  105.3 17.5 %step.1 = (f32[512,256]{1,0:T(8,128)}, f32[512,256]{1,0:T(8,128)}, f32[6400,256]{1,0:T(8,128)}, f32[256,2560]{1,0:T(8,128)}, f32[256,2560]{1,0:T(8,128)}, /*inde...) custom-call(bf16[4096,256]{1,0:T(8,128)(2,1)} %copy-done.3, ...), custom_call_target="tpu_custom_call" | custom-call | tf_op jit(solution)/shard_map/step/pallas_call | solution.py:1017
Async XLA Ops:
  1.4 1.7 %copy-start = (f32[256,2560]{1,0:T(8,128)S(1)}, f32[256,2560]{1,0:T(8,128)}, u32[]{:S(2)}) copy-start(f32[256,2560]{1,0:T(8,128)} %refs_5_.3) | copy-start | bytes 7864324
  3.1 1.2 copy-start.1
  4.3 1.0 copy-start.2
  5.4 1.0 copy-start.4
  6.4 1.0 copy-start.5
  7.5 0.7 copy-start.8
  8.2 0.8 copy-start.9
  101.9 1.4 %copy-start.3 = (bf16[4096,256]{1,0:T(8,128)(2,1)}, bf16[4096,256]{1,0:T(8,128)(2,1)S(1)}, u32[]{:S(2)}) copy-start(bf16[4096,256]{1,0:T(8,128)(2,1)S(1)} %get-tuple-element.35.refs_0_) | copy-start | bytes 6291460
  103.3 0.7 copy-start.6
  104.0 0.7 copy-start.7
  104.7 0.6 copy-start.10
where the time goes:
time: 123 us
  Pallas kernels  110 us (89%)
  local copies, waits for them, and re-layouts  11.7 us (10%)
    pallas_call x1, Pallas kernels, per_device(): pl.pallas_call(functools.partial(layer_kernel, names, sizes), out_shape=[...  92.9 us
    pallas_call x1, Pallas kernels, per_device(): pl.pallas_call(functools.partial(step_kernel, names2, float(rows * n_dp))...  17.5 us
    unnamed x23, local copies, waits for them, and re-layouts  11.7 us

commit v1 on v0

--- a/solution.py
+++ b/solution.py
@@ -109,13 +109,16 @@
     return jnp.concatenate([values, jnp.zeros((missing, values.shape[1]), values.dtype)], axis=0)
 
 
-def self_weights(q, k, blocks, causal):
-    k_blocks = jnp.concatenate([k] * HEADS, axis=0) * blocks
-    scores = jnp.where(causal, nt(q, k_blocks) * 0.125, LOWEST)
-    top = spread(head_reduce(scores, "max"))
-    raised = jnp.where(causal, jnp.exp(scores - top), 0.0)
-    total = spread(head_reduce(raised, "sum"))
-    return raised / total, k_blocks
+def self_weights(queries, keys, blocks, causal):
+    k_blocks = [jnp.concatenate([k] * HEADS, axis=0) * blocks for k in keys]
+    scores = [nt(q, kb) for q, kb in zip(queries, k_blocks)]
+    weights = []
+    for score in scores:
+        score = jnp.where(causal, score * 0.125, LOWEST)
+        top = spread(head_reduce(score, "max"))
+        raised = jnp.where(causal, jnp.exp(score - top), 0.0)
+        weights.append(raised / spread(head_reduce(raised, "sum")))
+    return weights, k_blocks
 
 
 class Names:
@@ -203,7 +206,7 @@
     w_up = lambda: r.rwb[:, 6 * width :]
 
     def self_forward(b):
-        group = 128
+        group = 256
 
         @pl.loop(0, part_rows // group)
         def _(g):
@@ -216,13 +219,11 @@
             r.qkv[span, :] = qkv
             causal = causal_mask()
             blocks = r.blocks[...]
-            mixed = []
-            for s in range(group // 64):
-                piece = qkv[s * 64 : s * 64 + 64, :]
-                q, k, v = (piece[:, i * width : (i + 1) * width] for i in range(3))
-                weights, _ = self_weights(q, k, blocks, causal)
-                v_blocks = jnp.concatenate([v] * HEADS, axis=0) * blocks
-                mixed.append(nn(half(weights), v_blocks))
+            pieces = [qkv[s * 64 : s * 64 + 64, :] for s in range(group // 64)]
+            q, k, v = ([p[:, i * width : (i + 1) * width] for p in pieces] for i in range(3))
+            v_blocks = [jnp.concatenate([x] * HEADS, axis=0) * blocks for x in v]
+            weights, _ = self_weights(q, k, blocks, causal)
+            mixed = [nn(half(w), vb) for w, vb in zip(weights, v_blocks)]
             o1 = half(jnp.concatenate(mixed, axis=0))
             r.o1[span, :] = o1
             x1 = x + nn(o1, w_so())
@@ -233,7 +234,7 @@
             r.qs[span, :] = half(nn(a2, w_cq()) * 0.125)
 
     def pair_forward(b):
-        batch = 4
+        batch = 8
         step = batch * slots
 
         @pl.loop(0, part_samples // batch)
@@ -254,25 +255,33 @@
         r.use[...] = jnp.where(kept | time_token, 1.0, 0.0)
 
     def cross_forward(b):
-        unroll = 2
+        unroll = 16
 
         @pl.loop(0, part_samples // unroll)
         def _(g):
-            for i in range(unroll):
-                s = b * part_samples + g * unroll + i
-                span = pl.ds(pl.multiple_of(s * H, H), H)
-                q = jnp.concatenate([r.qs[span, :]] * HEADS, axis=0) * r.heads_b[...]
+            picks = [b * part_samples + g * unroll + i for i in range(unroll)]
+            spans = [pl.ds(pl.multiple_of(s * H, H), H) for s in picks]
+            heads_b = r.heads_b[...]
+            scores = []
+            for s, span in zip(picks, spans):
+                q = jnp.concatenate([r.qs[span, :]] * HEADS, axis=0) * heads_b
+                scores.append(nt(q, r.kv[s, :, :width]))
+            weights = []
+            for s, span, score in zip(picks, spans, scores):
                 usable = jnp.broadcast_to(r.use[pl.ds(s, 1), :], (64, slots)) > 0.5
-                scores = jnp.where(usable, nt(q, r.kv[s, :, :width]), LOWEST)
-                top = jnp.max(scores, axis=1, keepdims=True)
-                raised = jnp.where(usable, jnp.exp(scores - top), 0.0)
+                score = jnp.where(usable, score, LOWEST)
+                top = jnp.max(score, axis=1, keepdims=True)
+                raised = jnp.where(usable, jnp.exp(score - top), 0.0)
                 total = jnp.sum(raised, axis=1, keepdims=True)
                 p = half(raised)
                 r.p[s] = p
-                mixed = nn(p, r.kv[s, :, width:]) * r.heads[...]
-                r.o_out[span, :] = half(sum(mixed[h * H : h * H + H, :] for h in range(HEADS)))
+                weights.append(p)
                 r.top[span, :] = lanes_of([top[h * H : h * H + H, :] for h in range(HEADS)])
                 r.total[span, :] = lanes_of([total[h * H : h * H + H, :] for h in range(HEADS)])
+            mixes = [nn(p, r.kv[s, :, width:]) for s, p in zip(picks, weights)]
+            for span, mixed in zip(spans, mixes):
+                mixed = mixed * r.heads[...]
+                r.o_out[span, :] = half(sum(mixed[h * H : h * H + H, :] for h in range(HEADS)))
 
     pending = []
 
@@ -317,11 +326,16 @@
                 )
 
     def middle(b):
+        mine = pl.ds(b * own, own)
+        me = own_span(b, c)
+        biases = hidden // width
+        cot = r.cot[me, :]
+        dz = half(cot)
+        r.dz[mine, :] = dz
+        grad_acts = [nt(dz, r.dwb[j * width : (j + 1) * width, :]) for j in range(biases)]
         for k in range(1, n_cond):
             for copy in flights["o", b, k]:
                 copy.wait_recv()
-        me = own_span(b, c)
-        mine = pl.ds(b * own, own)
         tops = [r.st_in[b, k, :8, :] for k in range(n_cond)]
         top = functools.reduce(jnp.maximum, tops)
         raised = [jnp.exp(t - top) for t in tops]
@@ -337,25 +351,28 @@
         unit, rate = unit_rows(x2)
         a3 = half(unit * vec(4) + vec(5))
         r.a3[mine, :] = a3
-        biases = hidden // width
-        cot = r.cot[me, :]
-        dz = half(cot)
-        r.dz[mine, :] = dz
+        ups = [slice(6 * width + j * width, 6 * width + (j + 1) * width) for j in range(biases)]
+        downs = [slice(j * width, (j + 1) * width) for j in range(biases)]
+        us = [nn(a3, r.rwb[:, cols]) for cols in ups]
+        acts, slopes = [], []
+        for j in range(biases):
+            u = us[j] + vec(6 + j)
+            below = 0.5 + 0.5 * lax.erf(u * (2.0**-0.5))
+            acts.append(half(u * below))
+            slopes.append(
+                below + u * (jnp.exp(-0.5 * u * u) * (1.0 / math.sqrt(2.0 * math.pi)))
+            )
+        dus = []
+        for j in range(biases):
+            du = half(grad_acts[j] * slopes[j])
+            r.du[mine, downs[j]] = du
+            dus.append(du)
+        da3 = sum(nt(du, r.rwb[:, cols]) for du, cols in zip(dus, ups))
+        for j in range(biases):
+            r.hb[mine, downs[j]] = acts[j]
+            add_vec(b, 6 + j, column_sum(wide(dus[j])))
         out = x2 + vec(6 + biases)
-        da3 = jnp.zeros((own, width), F32)
-        for j in range(biases):
-            cols = slice(6 * width + j * width, 6 * width + (j + 1) * width)
-            here = slice(j * width, (j + 1) * width)
-            u = nn(a3, r.rwb[:, cols]) + vec(6 + j)
-            below = 0.5 + 0.5 * lax.erf(u * (2.0**-0.5))
-            hb = half(u * below)
-            r.hb[mine, here] = hb
-            out = out + nn(hb, r.dwb[here, :])
-            slope = below + u * (jnp.exp(-0.5 * u * u) * (1.0 / math.sqrt(2.0 * math.pi)))
-            du = half(nt(dz, r.dwb[here, :]) * slope)
-            r.du[mine, here] = du
-            add_vec(b, 6 + j, column_sum(wide(du)))
-            da3 = da3 + nt(du, r.rwb[:, cols])
+        out = out + sum(nn(hb, r.dwb[here, :]) for hb, here in zip(acts, downs))
         r.out16[me, :] = half(out)
         add_vec(b, 6 + biases, column_sum(wide(dz)))
         add_vec(b, 4, column_sum(da3 * unit))
@@ -396,28 +413,39 @@
                 for copy in flights["do", b, k]:
                     copy.wait_recv()
             r.dl[own_span(b, owner), :] = pad_rows(r.dl_in[b, k], 128).T[:own, :]
-        unroll = 2
+        unroll = 16
 
         @pl.loop(0, part_samples // unroll)
         def _(g):
-            pairs = []
             first = b * part_samples + g * unroll
-            for i in range(unroll):
-                s = first + i
-                span = pl.ds(pl.multiple_of(s * H, H), H)
-                heads_b = r.heads_b[...]
-                q = jnp.concatenate([r.qs[span, :]] * HEADS, axis=0) * heads_b
-                grads = jnp.concatenate([r.do_in[span, :]] * HEADS, axis=0) * heads_b
+            picks = [first + i for i in range(unroll)]
+            spans = [pl.ds(pl.multiple_of(s * H, H), H) for s in picks]
+            heads_b = r.heads_b[...]
+            grads = [
+                jnp.concatenate([r.do_in[span, :]] * HEADS, axis=0) * heads_b for span in spans
+            ]
+            raws = [nt(grad, r.kv[s, :, width:]) for s, grad in zip(picks, grads)]
+            slopes = []
+            for s, span, raw in zip(picks, spans, raws):
                 dots = r.dl[span, :]
                 dots = jnp.concatenate([dots[:, h : h + 1] for h in range(HEADS)], axis=0)
-                p = r.p[s]
-                ds = half(wide(p) * (nt(grads, r.kv[s, :, width:]) - dots))
-                dq = nn(ds, r.kv[s, :, :width]) * r.heads[...]
+                slopes.append(half(wide(r.p[s]) * (raw - dots)))
+            backs = [nn(ds, r.kv[s, :, :width]) for s, ds in zip(picks, slopes)]
+            for span, dq in zip(spans, backs):
+                dq = dq * r.heads[...]
                 dq = sum(dq[h * H : h * H + H, :] for h in range(HEADS)) * 0.125
                 r.dq_out[span, :] = half(dq)
-                pairs.append(jnp.concatenate([tn(ds, q), tn(p, grads)], axis=1))
-            span = pl.ds(pl.multiple_of(first * slots, unroll * slots), unroll * slots)
-            r.dkv[span, :] = half(jnp.concatenate(pairs, axis=0))
+            for pair in range(unroll // 2):
+                keys, values = [], []
+                for i in (2 * pair, 2 * pair + 1):
+                    q = jnp.concatenate([r.qs[spans[i], :]] * HEADS, axis=0) * heads_b
+                    keys.append(tn(slopes[i], q))
+                    values.append(tn(r.p[picks[i]], grads[i]))
+                span = pl.ds(
+                    pl.multiple_of(first * slots + pair * 2 * slots, 2 * slots), 2 * slots
+                )
+                r.dkv[span, :width] = half(jnp.concatenate(keys, axis=0))
+                r.dkv[span, width:] = half(jnp.concatenate(values, axis=0))
 
     def send_query_grads(b):
         for k in range(1, n_cond):
@@ -446,19 +474,24 @@
         do1 = half(nt(dy1, w_so()))
         causal = causal_mask()
         blocks = r.blocks[...]
+        spans = [
+            pl.ds(pl.multiple_of(b * part_rows + c * own + s * 64, 64), 64)
+            for s in range(own // 64)
+        ]
+        q, k, v = (
+            [r.qkv[span, i * width : (i + 1) * width] for span in spans] for i in range(3)
+        )
+        grads = [do1[s * 64 : s * 64 + 64, :] for s in range(own // 64)]
+        v_blocks = [jnp.concatenate([x] * HEADS, axis=0) * blocks for x in v]
+        dps = [nt(grad, vb) for grad, vb in zip(grads, v_blocks)]
+        weights, k_blocks = self_weights(q, k, blocks, causal)
         pieces = []
-        for s in range(own // 64):
-            span = pl.ds(pl.multiple_of(b * part_rows + c * own + s * 64, 64), 64)
-            q, k, v = (r.qkv[span, i * width : (i + 1) * width] for i in range(3))
-            grads = do1[s * 64 : s * 64 + 64, :]
-            weights, k_blocks = self_weights(q, k, blocks, causal)
-            v_blocks = jnp.concatenate([v] * HEADS, axis=0) * blocks
-            dv = tn(half(weights), grads) * wide(blocks)
-            dp = nt(grads, v_blocks)
-            dots = spread(head_reduce(weights * dp, "sum"))
-            ds = half(weights * (dp - dots))
-            dq = nn(ds, k_blocks) * 0.125
-            dk = tn(ds, q) * wide(blocks)
+        for i in range(own // 64):
+            dv = tn(half(weights[i]), grads[i]) * wide(blocks)
+            dots = spread(head_reduce(weights[i] * dps[i], "sum"))
+            ds = half(weights[i] * (dps[i] - dots))
+            dq = nn(ds, k_blocks[i]) * 0.125
+            dk = tn(ds, q[i]) * wide(blocks)
             dk = sum(dk[h * 64 : h * 64 + 64, :] for h in range(HEADS)) * 0.125
             dv = sum(dv[h * 64 : h * 64 + 64, :] for h in range(HEADS))
             pieces.append(half(jnp.concatenate([dq, dk, dv], axis=1)))
@@ -497,10 +530,10 @@
             put_row(3 + j, tn(a1, r.dqkv[:, j * width : (j + 1) * width]))
 
     def pair_grads():
-        step = 2 * slots
+        step = 8 * slots
         r.gw[...] = jnp.zeros_like(r.gw)
 
-        @pl.loop(0, samples // 2)
+        @pl.loop(0, samples // 8)
         def _(g):
             span = pl.ds(pl.multiple_of(g * step, step), step)
             r.gw[...] += tn(r.mem[span, :], r.dkv[span, :])
@@ -971,7 +1004,7 @@
         "rsem": pltpu.SemaphoreType.DMA((96,)),
     }
     whole = pl.BlockSpec(memory_space=pltpu.VMEM)
-    far = pl.BlockSpec(memory_space=pl.ANY)
+    far = pl.BlockSpec(memory_space=pltpu.HBM)
     names = list(ins) + list(outs) + list(scratch) + list(sems)
     sizes = (rows, samples, slots, n_cond, n_dp, width)
     tot, vtot, dkv, out16, ga16 = pl.pallas_call(
@@ -981,10 +1014,10 @@
         out_specs=[whole] * len(outs),
         scratch_shapes=[pltpu.VMEM(*v) for v in scratch.values()] + list(sems.values()),
         compiler_params=pltpu.CompilerParams(
-            collective_id=0, has_side_effects=True, vmem_limit_bytes=44 * MIB
+            collective_id=0, has_side_effects=True, vmem_limit_bytes=32 * MIB
         ),
         name="layer",
-    )(*ins.values())
+    )(*(pltpu.with_memory_space_constraint(v, pltpu.HBM) for v in ins.values()))
 
     ins2 = {
         "tot": tot,
@@ -1021,7 +1054,7 @@
         out_specs=[far] * len(outs2),
         scratch_shapes=[pltpu.VMEM(v, F32) for v in outs2.values()]
         + [pltpu.VMEM(memory_weights.shape, BF), pltpu.SemaphoreType.DMA((32,))],
-        compiler_params=pltpu.CompilerParams(vmem_limit_bytes=60 * MIB),
+        compiler_params=pltpu.CompilerParams(vmem_limit_bytes=26 * MIB),
         name="step",
     )(*ins2.values())
     out, ga, gm = results[:3]

time: 123 us -> 88.2 us (0.72)
  Pallas kernels: 110 us -> 81.6 us
  local copies, waits for them, and re-layouts: 11.7 us -> 5.39 us
    pallas_call x1, Pallas kernels: 92.9 us -> 71.6 us  [per_device(): pl.pallas_call(functools.partial(layer_kernel, names, sizes), out_shape=[...]
    pallas_call x1, Pallas kernels: 17.5 us -> 10.1 us  [per_device(): pl.pallas_call(functools.partial(step_kernel, names2, float(rows * n_dp))...]
    unnamed x23 -> x25, local copies, waits for them, and re-layouts: 11.7 us -> 5.39 us
where the time goes in v1:
time: 88.2 us; the launch traced here: 88 us
  Pallas kernels  81.6 us (93%)
  local copies, waits for them, and re-layouts  5.39 us (6%)
  between operations  0.94 us (1%)
    pallas_call x1, Pallas kernels, per_device(): pl.pallas_call(functools.partial(layer_kernel, names, sizes), out_shape=[...  71.6 us
    pallas_call x1, Pallas kernels, per_device(): pl.pallas_call(functools.partial(step_kernel, names2, float(rows * n_dp))...  10.1 us
    unnamed x25, local copies, waits for them, and re-layouts  5.39 us

profile of v1, /device:TPU:1, one launch (start us, length us, event | category | flops | bytes accessed | tf_op | source)
XLA Modules:
  0.0 88.0 jit_solution(15618752238691940868)
XLA Ops:
  0.6 1.3 %copy.32.refs_3_ = s32[32,1]{1,0:T(8,128)} copy(s32[32,1]{0,1:T(1,128)} %param.19) | data formatting | bytes 256 | tf_op args[2]
  2.0 0.0 copy-start
  2.0 0.0 copy-start.1
  2.0 0.0 copy-start.2
  2.0 0.0 copy-start.4
  2.0 0.0 copy-start.5
  2.0 0.0 copy-start.7
  2.0 0.0 copy-start.9
  2.0 0.0 copy-start.10
  2.0 0.0 copy-start.11
  2.1 71.6 %layer.1 = (bf16[4096,256]{1,0:T(8,128)(2,1)S(1)}, f32[16,256]{1,0:T(8,128)S(1)}, bf16[6400,512]{1,0:T(8,128)(2,1)S(1)}, bf16[512,256]{1,0:T(8,128)(2,1)S(1)}, bf16[512,256]{1,0:T(8,128)(2,1)S(1)}) custom-call(f32[512,256]{1,0:T(8,128)} %refs_0_.1, bf16[6400,256]{1,0:T(8,128)(2,1)} %bitcast.2, s32[32,200]{1,0:T(8,128)} %refs_2_.1, s32[32,1]{1,0:T(8,128)} %copy.32.refs_3_, ...), custom_call_target="tpu_custom_call" | custom-call | tf_op jit(solution)/shard_map/layer/pallas_call | solution.py:1010
  73.6 0.0 copy-done
  73.7 0.0 copy-done.1
  73.7 0.0 copy-done.2
  73.7 0.0 copy-done.4
  73.7 0.0 copy-done.5
  73.7 0.0 copy-done.7
  73.7 0.0 copy-done.9
  73.7 0.0 copy-done.10
  73.7 0.0 copy-done.11
  73.7 0.0 copy-start.3
  73.7 1.7 %copy-done.3 = f32[256,2560]{1,0:T(8,128)S(1)} copy-done((f32[256,2560]{1,0:T(8,128)S(1)}, f32[256,2560]{1,0:T(8,128)}, u32[]{:S(2)}) %copy-start.3) | copy-done | bytes 2621464
  75.5 0.0 copy-start.6
  75.5 1.2 %copy-done.6 = f32[1024,256]{1,0:T(8,128)S(1)} copy-done((f32[1024,256]{1,0:T(8,128)S(1)}, f32[1024,256]{1,0:T(8,128)}, u32[]{:S(2)}) %copy-start.6) | copy-done | bytes 1048600
  76.7 0.0 copy-start.8
  76.7 1.0 %copy-done.8 = f32[256,512]{1,0:T(8,128)S(1)} copy-done((f32[256,512]{1,0:T(8,128)S(1)}, f32[256,512]{1,0:T(8,128)}, u32[]{:S(2)}) %copy-start.8) | copy-done | bytes 524312
  77.7 10.1 %step.1 = (f32[512,256]{1,0:T(8,128)}, f32[512,256]{1,0:T(8,128)}, f32[6400,256]{1,0:T(8,128)}, f32[256,2560]{1,0:T(8,128)}, f32[256,2560]{1,0:T(8,128)}, /*inde...) custom-call(bf16[4096,256]{1,0:T(8,128)(2,1)S(1)} %get-tuple-element, ...), custom_call_target="tpu_custom_call" | custom-call | tf_op jit(solution)/shard_map/step/pallas_call | solution.py:1050
Async XLA Ops:
  2.0 71.7 %copy-start = (f32[256,2560]{1,0:T(8,128)S(1)}, f32[256,2560]{1,0:T(8,128)}, u32[]{:S(2)}) copy-start(f32[256,2560]{1,0:T(8,128)} %refs_5_.3) | copy-start | bytes 7864324
  2.0 71.7 %copy-start.1 = (f32[1024,256]{1,0:T(8,128)S(1)}, f32[1024,256]{1,0:T(8,128)}, u32[]{:S(2)}) copy-start(f32[1024,256]{1,0:T(8,128)} %refs_7_.3) | copy-start | bytes 3145732
  2.0 71.7 %copy-start.2 = (f32[256,2560]{1,0:T(8,128)S(1)}, f32[256,2560]{1,0:T(8,128)}, u32[]{:S(2)}) copy-start(f32[256,2560]{1,0:T(8,128)} %refs_9_.1) | copy-start | bytes 7864324
  2.0 71.7 %copy-start.4 = (f32[256,512]{1,0:T(8,128)S(1)}, f32[256,512]{1,0:T(8,128)}, u32[]{:S(2)}) copy-start(f32[256,512]{1,0:T(8,128)} %refs_6_.3) | copy-start | bytes 1572868
  2.0 71.7 %copy-start.5 = (f32[1024,256]{1,0:T(8,128)S(1)}, f32[1024,256]{1,0:T(8,128)}, u32[]{:S(2)}) copy-start(f32[1024,256]{1,0:T(8,128)} %refs_11_.1) | copy-start | bytes 3145732
  2.0 71.7 %copy-start.7 = (f32[256,512]{1,0:T(8,128)S(1)}, f32[256,512]{1,0:T(8,128)}, u32[]{:S(2)}) copy-start(f32[256,512]{1,0:T(8,128)} %refs_10_.1) | copy-start | bytes 1572868
  2.0 71.7 %copy-start.9 = (f32[11,256]{1,0:T(8,128)S(1)}, f32[11,256]{1,0:T(8,128)}, u32[]{:S(2)}) copy-start(f32[11,256]{1,0:T(8,128)} %refs_8_.3) | copy-start | bytes 33796
  2.0 71.7 %copy-start.10 = (f32[11,256]{1,0:T(8,128)S(1)}, f32[11,256]{1,0:T(8,128)}, u32[]{:S(2)}) copy-start(f32[11,256]{1,0:T(8,128)} %refs_12_.1) | copy-start | bytes 33796
  2.0 71.7 %copy-start.11 = (f32[11,256]{1,0:T(8,128)S(1)}, f32[11,256]{1,0:T(8,128)}, u32[]{:S(2)}) copy-start(f32[11,256]{1,0:T(8,128)} %refs_16_.1) | copy-start | bytes 33796
  73.7 1.7 %copy-start.3 = (f32[256,2560]{1,0:T(8,128)S(1)}, f32[256,2560]{1,0:T(8,128)}, u32[]{:S(2)}) copy-start(f32[256,2560]{1,0:T(8,128)} %refs_13_.1) | copy-start | bytes 7864324
  75.5 1.2 %copy-start.6 = (f32[1024,256]{1,0:T(8,128)S(1)}, f32[1024,256]{1,0:T(8,128)}, u32[]{:S(2)}) copy-start(f32[1024,256]{1,0:T(8,128)} %refs_15_.1) | copy-start | bytes 3145732
  76.7 1.0 %copy-start.8 = (f32[256,512]{1,0:T(8,128)S(1)}, f32[256,512]{1,0:T(8,128)}, u32[]{:S(2)}) copy-start(f32[256,512]{1,0:T(8,128)} %refs_14_.1) | copy-start | bytes 1572868

commit v2 on v1

v2 whole, which is shorter than its diff:
```python
import functools
import math

import jax
import jax.numpy as jnp
from jax import lax
from jax.experimental import pallas as pl
from jax.experimental.pallas import tpu as pltpu
from jax.sharding import PartitionSpec as P

HEADS = 4
H = 16
PATCHES = 196
STEP = 10
INERTIA = 0.9
STEP_RATE = 1.0
LOWEST = -1e30
NB = 2
MESH = pl.DeviceIdType.MESH
MIB = 2**20
BF = jnp.bfloat16
F32 = jnp.float32


def half(values):
    return values.astype(BF)


def wide(values):
    return values.astype(F32)


def nn(a, b):
    return jnp.dot(a, b, preferred_element_type=F32)


def nt(a, b):
    return lax.dot_general(a, b, (((1,), (1,)), ((), ())), preferred_element_type=F32)


def tn(a, b):
    return lax.dot_general(a, b, (((0,), (0,)), ((), ())), preferred_element_type=F32)


def unit_rows(values):
    centered = values - jnp.mean(values, axis=-1, keepdims=True)
    rate = lax.rsqrt(jnp.mean(centered * centered, axis=-1, keepdims=True) + 1e-05)
    return centered * rate, rate


def unit_back(grad, unit, rate):
    return rate * (
        grad
        - jnp.mean(grad, axis=-1, keepdims=True)
        - unit * jnp.mean(grad * unit, axis=-1, keepdims=True)
    )


def column_sum(values):
    return jnp.sum(values, axis=0, keepdims=True)


def head_columns(table, first):
    rows = table.shape[0]
    low_lane = lax.broadcasted_iota(jnp.int32, (rows, 128), 1) < 64
    cols = [table[:, first + h : first + h + 1] for h in range(HEADS)]
    return jnp.concatenate(
        [jnp.where(low_lane, cols[0], cols[1]), jnp.where(low_lane, cols[2], cols[3])], axis=1
    )


def head_reduce(values, kind):
    rows = values.shape[0]
    low_lane = lax.broadcasted_iota(jnp.int32, (rows, 128), 1) < 64
    fill = LOWEST if kind == "max" else 0.0
    cols = []
    for pair in range(2):
        part = values[:, pair * 128 : pair * 128 + 128]
        for keep_low in (True, False):
            picked = jnp.where(low_lane == keep_low, part, fill)
            if kind == "max":
                cols.append(jnp.max(picked, axis=1, keepdims=True))
            else:
                cols.append(jnp.sum(picked, axis=1, keepdims=True))
    return cols


def spread(cols):
    rows = cols[0].shape[0]
    low_lane = lax.broadcasted_iota(jnp.int32, (rows, 128), 1) < 64
    return jnp.concatenate(
        [jnp.where(low_lane, cols[0], cols[1]), jnp.where(low_lane, cols[2], cols[3])], axis=1
    )


def lanes_of(cols):
    rows = cols[0].shape[0]
    lane = lax.broadcasted_iota(jnp.int32, (rows, 128), 1)
    table = jnp.zeros((rows, 128), F32)
    for h, col in enumerate(cols):
        table = jnp.where(lane == h, col, table)
    return table


def pad_rows(values, rows):
    missing = rows - values.shape[0]
    if missing == 0:
        return values
    return jnp.concatenate([values, jnp.zeros((missing, values.shape[1]), values.dtype)], axis=0)


def self_weights(queries, keys, blocks, causal, beside=lambda: None):
    k_blocks = [jnp.concatenate([k] * HEADS, axis=0) * blocks for k in keys]
    scores = [nt(q, kb) for q, kb in zip(queries, k_blocks)]
    beside()
    weights = []
    for score in scores:
        score = jnp.where(causal, score * 0.125, LOWEST)
        top = spread(head_reduce(score, "max"))
        raised = jnp.where(causal, jnp.exp(score - top), 0.0)
        weights.append(raised / spread(head_reduce(raised, "sum")))
    return weights, k_blocks


class Names:
    pass


def layer_kernel(names, sizes, *refs):
    r = Names()
    for name, ref in zip(names, refs, strict=True):
        setattr(r, name, ref)
    rows, samples, slots, n_cond, n_dp, width = sizes
    hidden = r.dw.shape[0]
    part_rows = rows // NB
    own = part_rows // n_cond
    part_samples = samples // NB
    c = lax.axis_index("cond")
    d = lax.axis_index("dp")

    def peer(k):
        return (d, lax.rem(c + k, n_cond))

    core = lax.rem(c, 2)
    side_x = lax.rem(d, 2)
    side_y = c // 2
    plane = side_x + 2 * side_y
    line = d // 2
    n_line = n_dp // 2
    core_peer = (d, c + 1 - 2 * core)
    chip_peer = (d, lax.rem(c + 2, n_cond))

    def plane_place(k):
        x = 1 - side_x if k & 1 else side_x
        y = 1 - side_y if k & 2 else side_y
        return x + 2 * y

    def plane_peer(k):
        return (
            d + 1 - 2 * side_x if k & 1 else d,
            lax.rem(c + 2, n_cond) if k & 2 else c,
        )

    def line_place(k):
        return lax.rem(line + k, n_line)

    def line_peer(k):
        return (2 * line_place(k) + side_x, c)

    barrier = pltpu.get_barrier_semaphore()
    friends = [peer(k) for k in range(1, n_cond)]
    friends += [plane_peer(k) for k in (1, 3)]
    friends += [line_peer(k) for k in range(1, n_line)]
    for friend in friends:
        pl.semaphore_signal(barrier, inc=1, device_id=friend, device_id_type=MESH)

    loads = {}

    def load(name, src, dst, at):
        copy = pltpu.make_async_copy(src, dst, r.load_sem.at[at])
        copy.start()
        loads[name] = copy

    mem_parts = 4
    mem_rows = samples * slots // mem_parts

    def load_memory(i):
        span = pl.ds(i * mem_rows, mem_rows)
        load(f"mem{i}", r.mem_h.at[span], r.mem.at[span], 8 + i)

    load("mw", r.mw_h, r.mw, 3)
    load_memory(0)
    load("act", r.act_h, r.act, 0)
    load("vec", r.vec_h, r.vec, 2)
    load("rw", r.rw_h, r.rw, 1)
    load_memory(1)
    load("mask", r.mask_h, r.mask, 4)
    load("flag", r.flag_h, r.flag, 5)
    load("dw", r.dw_h, r.dw, 6)
    load("cot", r.cot_h, r.cot, 7)
    load_memory(2)
    load_memory(3)

    def load_moments():
        for i, name in enumerate(("m_r", "m_d", "m_p", "a_r", "a_d", "a_p")):
            load(name, getattr(r, name + "_h"), getattr(r, name), 16 + i)

    lane256 = lax.broadcasted_iota(jnp.int32, (256, 256), 1)
    row256 = lax.broadcasted_iota(jnp.int32, (256, 256), 0)
    r.blocks[...] = half(jnp.where(lane256 // 64 == row256 // 64, 1.0, 0.0))
    lane64 = lax.broadcasted_iota(jnp.int32, (64, 256), 1)
    row64 = lax.broadcasted_iota(jnp.int32, (64, 256), 0)
    r.heads[...] = jnp.where(lane64 // 64 == row64 // 16, 1.0, 0.0)
    r.heads_b[...] = half(r.heads[...])

    def causal_mask():
        key = lax.rem(lane64, 64)
        return (key // H == row64 // H) & (key <= row64)

    def vec(i):
        return r.vec[i : i + 1, :]

    w_qkv = lambda: r.rwb[:, : 3 * width]
    w_so = lambda: r.rwb[:, 3 * width : 4 * width]
    w_cq = lambda: r.rwb[:, 4 * width : 5 * width]
    w_co = lambda: r.rwb[:, 5 * width : 6 * width]
    w_up = lambda: r.rwb[:, 6 * width :]

    def pair_forward(first):
        span = pl.ds(pl.multiple_of(first * slots, 2 * slots), 2 * slots)
        kv = nn(r.mem[span, :], r.mwb[...])
        for s in range(2):
            r.kv[first + s] = half(kv[s * slots : (s + 1) * slots, :])

    def first_forward(b, waiting):
        def fill(count):
            for _ in range(min(count, len(waiting))):
                pair_forward(waiting.pop(0))

        span = pl.ds(b * part_rows, part_rows)
        x = r.act[span, :]
        unit, _ = unit_rows(x)
        a1 = half(unit * vec(0) + vec(1))
        r.a1[span, :] = a1
        fill(1)
        qkv = half(nn(a1, w_qkv()))
        r.qkv[span, :] = qkv
        fill(1)
        causal = causal_mask()
        blocks = r.blocks[...]
        pieces = [qkv[s * 64 : s * 64 + 64, :] for s in range(part_rows // 64)]
        q, k, v = ([p[:, i * width : (i + 1) * width] for p in pieces] for i in range(3))
        v_blocks = [jnp.concatenate([x] * HEADS, axis=0) * blocks for x in v]
        weights, _ = self_weights(q, k, blocks, causal, lambda: fill(2))
        mixed = [nn(half(w), vb) for w, vb in zip(weights, v_blocks)]
        o1 = half(jnp.concatenate(mixed, axis=0))
        r.o1[span, :] = o1
        fill(1)
        x1 = x + nn(o1, w_so())
        r.x1[span, :] = x1
        fill(2)
        unit2, _ = unit_rows(x1)
        a2 = half(unit2 * vec(2) + vec(3))
        r.a2[span, :] = a2
        r.qs[span, :] = half(nn(a2, w_cq()) * 0.125)
        fill(len(waiting))

    def usable_rows():
        position = lax.broadcasted_iota(jnp.int32, (samples, slots), 1)
        square = (samples, samples)
        diagonal = lax.broadcasted_iota(jnp.int32, square, 0) == lax.broadcasted_iota(
            jnp.int32, square, 1
        )
        counts = jnp.where(diagonal, jnp.broadcast_to(r.flag[...], square), 0)
        counts = jnp.sum(counts.astype(F32), axis=1, keepdims=True)
        kept = (position.astype(F32) < counts) & (r.mask[...] == 1)
        time_token = (position == PATCHES) & (c == 0)
        r.use[...] = jnp.where(kept | time_token, 1.0, 0.0)

    def cross_forward(b):
        unroll = 16

        @pl.loop(0, part_samples // unroll)
        def _(g):
            picks = [b * part_samples + g * unroll + i for i in range(unroll)]
            spans = [pl.ds(pl.multiple_of(s * H, H), H) for s in picks]
            heads_b = r.heads_b[...]
            scores = []
            for s, span in zip(picks, spans):
                q = jnp.concatenate([r.qs[span, :]] * HEADS, axis=0) * heads_b
                scores.append(nt(q, r.kv[s, :, :width]))
            weights = []
            for s, span, score in zip(picks, spans, scores):
                usable = jnp.broadcast_to(r.use[pl.ds(s, 1), :], (64, slots)) > 0.5
                score = jnp.where(usable, score, LOWEST)
                top = jnp.max(score, axis=1, keepdims=True)
                raised = jnp.where(usable, jnp.exp(score - top), 0.0)
                total = jnp.sum(raised, axis=1, keepdims=True)
                p = half(raised)
                r.p[s] = p
                weights.append(p)
                r.top[span, :] = lanes_of([top[h * H : h * H + H, :] for h in range(HEADS)])
                r.total[span, :] = lanes_of([total[h * H : h * H + H, :] for h in range(HEADS)])
            mixes = [nn(p, r.kv[s, :, width:]) for s, p in zip(picks, weights)]
            for span, mixed in zip(spans, mixes):
                mixed = mixed * r.heads[...]
                r.o_out[span, :] = half(sum(mixed[h * H : h * H + H, :] for h in range(HEADS)))

    pending = []

    def send(src, dst, at, to):
        copy = pltpu.make_async_remote_copy(
            src_ref=src,
            dst_ref=dst,
            send_sem=r.ssem.at[at],
            recv_sem=r.rsem.at[at],
            device_id=to,
            device_id_type=MESH,
        )
        copy.start()
        pending.append(copy)
        return copy

    def own_span(b, owner):
        return pl.ds(pl.multiple_of(b * part_rows + owner * own, own), own)

    flights = {}

    def send_mixed(b):
        for k in range(n_cond):
            owner = lax.rem(c + k, n_cond)
            span = own_span(b, owner)
            stats = jnp.concatenate(
                [
                    pad_rows(r.top[span, :], 128).T[:8, :],
                    pad_rows(r.total[span, :], 128).T[:8, :],
                ],
                axis=0,
            )
            if k == 0:
                r.st_in[b, 0] = stats
                r.o_in[b, 0] = r.o_out[span, :]
            else:
                r.st_out[b, k] = stats
                at = (b * n_cond + k) * 2
                flights["o", b, k] = (
                    send(r.st_out.at[b, k], r.st_in.at[b, k], at, peer(k)),
                    send(r.o_out.at[span, :], r.o_in.at[b, k], at + 1, peer(k)),
                )

    def middle(b):
        mine = pl.ds(b * own, own)
        me = own_span(b, c)
        biases = hidden // width
        cot = r.cot[me, :]
        dz = half(cot)
        r.dz[mine, :] = dz
        grad_acts = [nt(dz, r.dwb[j * width : (j + 1) * width, :]) for j in range(biases)]
        for k in range(1, n_cond):
            for copy in flights["o", b, k]:
                copy.wait_recv()
        tops = [r.st_in[b, k, :8, :] for k in range(n_cond)]
        top = functools.reduce(jnp.maximum, tops)
        raised = [jnp.exp(t - top) for t in tops]
        total = sum(w * r.st_in[b, k, 8:, :] for k, w in enumerate(raised))
        total = jnp.maximum(total, 0.5)
        shares = [w / total for w in raised]
        table = pad_rows(jnp.concatenate(shares, axis=0), 128).T[:own, :]
        spreads = [head_columns(table, 8 * k) for k in range(n_cond)]
        o2 = sum(spreads[k] * wide(r.o_in[b, k]) for k in range(n_cond))
        o2b = half(o2)
        r.o2[mine, :] = o2b
        x2 = r.x1[me, :] + nn(o2b, w_co())
        unit, rate = unit_rows(x2)
        a3 = half(unit * vec(4) + vec(5))
        r.a3[mine, :] = a3
        ups = [slice(6 * width + j * width, 6 * width + (j + 1) * width) for j in range(biases)]
        downs = [slice(j * width, (j + 1) * width) for j in range(biases)]
        us = [nn(a3, r.rwb[:, cols]) for cols in ups]
        acts, slopes = [], []
        for j in range(biases):
            u = us[j] + vec(6 + j)
            below = 0.5 + 0.5 * lax.erf(u * (2.0**-0.5))
            acts.append(half(u * below))
            slopes.append(
                below + u * (jnp.exp(-0.5 * u * u) * (1.0 / math.sqrt(2.0 * math.pi)))
            )
        dus = []
        for j in range(biases):
            du = half(grad_acts[j] * slopes[j])
            r.du[mine, downs[j]] = du
            dus.append(du)
        da3 = sum(nt(du, r.rwb[:, cols]) for du, cols in zip(dus, ups))
        dx2 = cot + unit_back(da3 * vec(4), unit, rate)
        r.dx2[mine, :] = dx2
        dy = half(dx2)
        r.dy2[mine, :] = dy
        do2 = wide(half(nt(dy, w_co())))
        delta = lanes_of(head_reduce(do2 * wide(o2b), "sum"))
        delta = pad_rows(delta, 128).T[:8, :]
        for k in range(n_cond):
            grads = half(do2 * spreads[k])
            dots = delta * shares[k]
            if k == 0:
                r.do_in[me, :] = grads
                r.dl_in[b, 0] = dots
            else:
                r.do_out[b, k] = grads
                r.dl_out[b, k] = dots
                at = (NB * n_cond + b * n_cond + k) * 2
                to = peer(n_cond - k)
                flights["do", b, k] = (
                    send(r.dl_out.at[b, k], r.dl_in.at[b, k], at, to),
                    send(r.do_out.at[b, k], r.do_in.at[me, :], at + 1, to),
                )
        for j in range(biases):
            r.hb[mine, downs[j]] = acts[j]
            add_vec(b, 6 + j, column_sum(wide(dus[j])))
        out = x2 + vec(6 + biases)
        out = out + sum(nn(hb, r.dwb[here, :]) for hb, here in zip(acts, downs))
        r.out16[me, :] = half(out)
        add_vec(b, 6 + biases, column_sum(wide(dz)))
        add_vec(b, 4, column_sum(da3 * unit))
        add_vec(b, 5, column_sum(da3))

    def add_vec(b, i, values):
        if b == 0:
            r.vg[i : i + 1, :] = values
        else:
            r.vg[i : i + 1, :] += values

    def cross_backward(b):
        for k in range(n_cond):
            owner = lax.rem(c + k, n_cond)
            if k:
                for copy in flights["do", b, k]:
                    copy.wait_recv()
            r.dl[own_span(b, owner), :] = pad_rows(r.dl_in[b, k], 128).T[:own, :]
        unroll = 16

        @pl.loop(0, part_samples // unroll)
        def _(g):
            first = b * part_samples + g * unroll
            picks = [first + i for i in range(unroll)]
            spans = [pl.ds(pl.multiple_of(s * H, H), H) for s in picks]
            heads_b = r.heads_b[...]
            grads = [
                jnp.concatenate([r.do_in[span, :]] * HEADS, axis=0) * heads_b for span in spans
            ]
            raws = [nt(grad, r.kv[s, :, width:]) for s, grad in zip(picks, grads)]
            slopes = []
            for s, span, raw in zip(picks, spans, raws):
                dots = r.dl[span, :]
                dots = jnp.concatenate([dots[:, h : h + 1] for h in range(HEADS)], axis=0)
                ds = half(wide(r.p[s]) * (raw - dots))
                r.ds[s] = ds
                slopes.append(ds)
            backs = [nn(ds, r.kv[s, :, :width]) for s, ds in zip(picks, slopes)]
            for span, dq in zip(spans, backs):
                dq = dq * r.heads[...]
                dq = sum(dq[h * H : h * H + H, :] for h in range(HEADS)) * 0.125
                r.dq_out[span, :] = half(dq)

    def cross_backward_pairs(b):
        unroll = 16

        @pl.loop(0, part_samples // unroll)
        def _(g):
            first = b * part_samples + g * unroll
            picks = [first + i for i in range(unroll)]
            spans = [pl.ds(pl.multiple_of(s * H, H), H) for s in picks]
            heads_b = r.heads_b[...]
            for pair in range(unroll // 2):
                keys, values = [], []
                for i in (2 * pair, 2 * pair + 1):
                    q = jnp.concatenate([r.qs[spans[i], :]] * HEADS, axis=0) * heads_b
                    grad = jnp.concatenate([r.do_in[spans[i], :]] * HEADS, axis=0) * heads_b
                    keys.append(tn(r.ds[picks[i]], q))
                    values.append(tn(r.p[picks[i]], grad))
                span = pl.ds(
                    pl.multiple_of(first * slots + pair * 2 * slots, 2 * slots), 2 * slots
                )
                r.dkv[span, :width] = half(jnp.concatenate(keys, axis=0))
                r.dkv[span, width:] = half(jnp.concatenate(values, axis=0))

    def send_query_grads(b):
        for k in range(1, n_cond):
            owner = lax.rem(c + k, n_cond)
            at = 4 * NB * n_cond + b * n_cond + k
            flights["dq", b, k] = send(
                r.dq_out.at[own_span(b, owner), :], r.dq_in.at[b, k], at, peer(k)
            )

    def self_backward(b):
        me = own_span(b, c)
        mine = pl.ds(b * own, own)
        total = wide(r.dq_out[me, :])
        for k in range(1, n_cond):
            flights["dq", b, k].wait_recv()
            total = total + wide(r.dq_in[b, k])
        dqc = half(total)
        r.dqc[mine, :] = dqc
        da2 = nt(dqc, w_cq())
        unit2, rate2 = unit_rows(r.x1[me, :])
        dx1 = r.dx2[mine, :] + unit_back(da2 * vec(2), unit2, rate2)
        dy1 = half(dx1)
        r.dy1[mine, :] = dy1
        do1 = half(nt(dy1, w_so()))
        causal = causal_mask()
        blocks = r.blocks[...]
        spans = [
            pl.ds(pl.multiple_of(b * part_rows + c * own + s * 64, 64), 64)
            for s in range(own // 64)
        ]
        q, k, v = (
            [r.qkv[span, i * width : (i + 1) * width] for span in spans] for i in range(3)
        )
        grads = [do1[s * 64 : s * 64 + 64, :] for s in range(own // 64)]
        v_blocks = [jnp.concatenate([x] * HEADS, axis=0) * blocks for x in v]
        dps = [nt(grad, vb) for grad, vb in zip(grads, v_blocks)]
        weights, k_blocks = self_weights(q, k, blocks, causal)
        pieces = []
        for i in range(own // 64):
            dv = tn(half(weights[i]), grads[i]) * wide(blocks)
            dots = spread(head_reduce(weights[i] * dps[i], "sum"))
            ds = half(weights[i] * (dps[i] - dots))
            dq = nn(ds, k_blocks[i]) * 0.125
            dk = tn(ds, q[i]) * wide(blocks)
            dk = sum(dk[h * 64 : h * 64 + 64, :] for h in range(HEADS)) * 0.125
            dv = sum(dv[h * 64 : h * 64 + 64, :] for h in range(HEADS))
            pieces.append(half(jnp.concatenate([dq, dk, dv], axis=1)))
        dqkv = jnp.concatenate(pieces, axis=0)
        r.dqkv[mine, :] = dqkv
        r.dx1[mine, :] = dx1
        add_vec(b, 2, column_sum(da2 * unit2))
        add_vec(b, 3, column_sum(da2))

    def self_backward_rest(b):
        me = own_span(b, c)
        mine = pl.ds(b * own, own)
        da1 = nt(r.dqkv[mine, :], w_qkv())
        unit1, rate1 = unit_rows(r.act[me, :])
        add_vec(b, 0, column_sum(da1 * unit1))
        add_vec(b, 1, column_sum(da1))
        r.ga16[me, :] = half(r.dx1[mine, :] + unit_back(da1 * vec(0), unit1, rate1))

    pair_first = 2 * hidden + 6 * width
    layout = {
        "up": (0, hidden),
        "down": (hidden, hidden),
        "row1": (2 * hidden, 2 * width),
        "row2": (2 * hidden + 2 * width, 2 * width),
        "row3": (2 * hidden + 4 * width, 2 * width),
        "pair": (pair_first, 2 * width),
    }
    set_at = {name: 5 * NB * n_cond + 10 * i for i, name in enumerate(layout)}
    vec_at = 5 * NB * n_cond + 10 * len(layout)
    share_at = vec_at + 5

    def owned(ref):
        return jnp.concatenate([ref[own_span(b, c), :] for b in range(NB)], axis=0)

    def up_grads():
        for j in range(hidden // width):
            here = slice(j * width, (j + 1) * width)
            r.g[here, :] = half(tn(r.a3[...], r.du[:, here]))

    def down_grads():
        for j in range(hidden // width):
            here = slice(j * width, (j + 1) * width)
            at = hidden + j * width
            r.g[at : at + width, :] = half(tn(r.hb[:, here], r.dz[...]))

    def put_row(j, values):
        first = 2 * hidden + j * width
        r.g[first : first + width, :] = half(values)

    def row1_grads():
        put_row(0, tn(r.o2[...], r.dy2[...]))
        put_row(1, tn(owned(r.a2), r.dqc[...]))

    def row2_grads():
        put_row(2, tn(owned(r.o1), r.dy1[...]))
        put_row(3, tn(owned(r.a1), r.dqkv[:, :width]))

    def row3_grads():
        for j in (1, 2):
            put_row(3 + j, tn(owned(r.a1), r.dqkv[:, j * width : (j + 1) * width]))

    def pair_grads(b):
        batch = 8
        step = batch * slots
        if b == 0:
            r.gw[...] = jnp.zeros_like(r.gw)

        @pl.loop(0, part_samples // batch)
        def _(g):
            span = pl.ds(pl.multiple_of((b * part_samples + g * batch) * slots, step), step)
            r.gw[...] += tn(r.mem[span, :], r.dkv[span, :])

        if b == NB - 1:
            for side in range(2):
                r.g[pair_first + side * width : pair_first + (side + 1) * width, :] = half(
                    r.gw[:, side * width : (side + 1) * width]
                )

    def set_sizes(name):
        first, count = layout[name]
        eighth = count // 8
        piece = max(16, eighth // n_line)
        return first, count // 2, eighth, piece, eighth // piece

    def at_rows(start, count):
        return pl.ds(pl.multiple_of(start, 16), count)

    def start(src, dst, at, to):
        pltpu.make_async_remote_copy(
            src_ref=src,
            dst_ref=dst,
            send_sem=r.ssem.at[at],
            recv_sem=r.rsem.at[at],
            device_id=to,
            device_id_type=MESH,
        ).start()

    def wait_rows(ref, count, at, which):
        view = ref.at[pl.ds(0, count), :]
        copy = pltpu.make_async_remote_copy(
            src_ref=view,
            dst_ref=view,
            send_sem=r.ssem.at[at],
            recv_sem=r.rsem.at[at],
            device_id=core_peer,
            device_id_type=MESH,
        )
        copy.wait_recv() if which == "recv" else copy.wait_send()

    def guard(full, cond, body):
        body() if full else pl.when(cond)(body)

    def wait_others(owners, piece, ref, at, which):
        if owners == n_line:
            wait_rows(ref, (n_line - 1) * piece, at, which)
        else:
            if owners > 1:
                pl.when(line < owners)(
                    lambda: wait_rows(ref, (owners - 1) * piece, at, which)
                )
            pl.when(line >= owners)(lambda: wait_rows(ref, owners * piece, at, which))

    def reduce_core(name):
        first, two, eighth, piece, owners = set_sizes(name)
        flights[name, 0] = send(
            r.g.at[at_rows(first + (1 - core) * two, two), :],
            r.rc.at[at_rows(first // 2, two), :],
            set_at[name],
            core_peer,
        )

    def reduce_plane(name):
        first, two, eighth, piece, owners = set_sizes(name)
        flights[name, 0].wait_recv()
        base = first // 2
        for k in (3, 1, 2, 0):
            span = at_rows(base + plane_place(k) * eighth, eighth)
            here = at_rows(first + core * two + plane_place(k) * eighth, eighth)
            r.rc[span, :] = half(wide(r.rc[span, :]) + wide(r.g[here, :]))
            if k:
                flights[name, k] = send(
                    r.rc.at[span, :],
                    r.rp.at[k - 1, pl.ds(first // 8, eighth), :],
                    set_at[name] + k,
                    plane_peer(k),
                )

    def reduce_line(name):
        first, two, eighth, piece, owners = set_sizes(name)
        total = wide(r.rc[at_rows(first // 2 + plane * eighth, eighth), :])
        base = first // 8
        for k in range(1, 4):
            flights[name, k].wait_recv()
            total = total + wide(r.rp[k - 1, base : base + eighth, :])
        r.ps[base : base + eighth, :] = half(total)
        for k in range(1, n_line):

            def go(k=k):
                start(
                    r.ps.at[at_rows(base + line_place(k) * piece, piece), :],
                    r.rz.at[pl.ds((layout_at(name) * n_line + k) * biggest, piece), :],
                    set_at[name] + 4,
                    line_peer(k),
                )

            guard(owners == n_line, line_place(k) < owners, go)

    biggest = max(set_sizes(name)[3] for name in layout)

    def layout_at(name):
        return list(layout).index(name)

    def own_eighth(name):
        first, two, eighth, piece, owners = set_sizes(name)
        return first + core * two + plane * eighth

    def gather_line(name):
        first, two, eighth, piece, owners = set_sizes(name)

        def finish():
            wait_rows(r.rz, (n_line - 1) * piece, set_at[name] + 4, "recv")
            total = wide(r.ps[at_rows(first // 8 + line * piece, piece), :])
            for k in range(1, n_line):
                at = (layout_at(name) * n_line + k) * biggest
                total = total + wide(r.rz[at : at + piece, :])
            here = at_rows(own_eighth(name) + line * piece, piece)
            r.tot[here, :] = half(total)
            for k in range(1, n_line):
                start(r.tot.at[here, :], r.tot.at[here, :], set_at[name] + 5, line_peer(k))

        guard(owners == n_line, line < owners, finish)

    def gather_plane(name):
        first, two, eighth, piece, owners = set_sizes(name)
        wait_others(owners, piece, r.tot, set_at[name] + 5, "recv")
        span = at_rows(own_eighth(name), eighth)
        for k in (3, 1, 2):
            flights[name, 5 + k] = send(
                r.tot.at[span, :], r.tot.at[span, :], set_at[name] + 5 + k, plane_peer(k)
            )

    def gather_core(name):
        first, two, eighth, piece, owners = set_sizes(name)
        for k in range(1, 4):
            flights[name, 5 + k].wait_recv()
        span = at_rows(first + core * two, two)
        flights[name, 9] = send(
            r.tot.at[span, :], r.tot.at[span, :], set_at[name] + 9, core_peer
        )

    def end_set(name):
        first, two, eighth, piece, owners = set_sizes(name)
        flights[name, 9].wait_recv()
        wait_others(owners, piece, r.ps, set_at[name] + 4, "send")
        guard(
            owners == n_line,
            line < owners,
            lambda: wait_rows(r.tot, (n_line - 1) * piece, set_at[name] + 5, "send"),
        )

    def small_core():
        r.v2[pl.ds(core, 1)] = r.vg[...][None]
        flights["v", 0] = send(r.v2.at[core], r.v2.at[core], vec_at, core_peer)

    def small_plane():
        flights["v", 0].wait_recv()
        r.v4[pl.ds(plane, 1)] = (r.v2[0] + r.v2[1])[None]
        for k in (3, 1, 2):
            flights["v", k] = send(
                r.v4.at[plane], r.v4.at[plane], vec_at + k, plane_peer(k)
            )

    def small_line():
        for k in range(1, 4):
            flights["v", k].wait_recv()
        r.vz[pl.ds(line, 1)] = (r.v4[0] + r.v4[1] + r.v4[2] + r.v4[3])[None]
        for k in range(1, n_line):
            start(r.vz.at[line], r.vz.at[line], vec_at + 4, line_peer(k))

    def small_wait(which):
        view = r.vz.at[pl.ds(0, n_line - 1)]
        copy = pltpu.make_async_remote_copy(
            src_ref=view,
            dst_ref=view,
            send_sem=r.ssem.at[vec_at + 4],
            recv_sem=r.rsem.at[vec_at + 4],
            device_id=core_peer,
            device_id_type=MESH,
        )
        copy.wait_recv() if which == "recv" else copy.wait_send()

    def small_end():
        small_wait("recv")
        total = r.vz[0]
        for k in range(1, n_line):
            total = total + r.vz[k]
        r.vtot[...] = total
        small_wait("send")

    def share(i, ref, b):
        at = share_at + 3 * (i * NB + b)
        span = own_span(b, c)
        flights["s", i, b, 0] = send(ref.at[span, :], ref.at[span, :], at, chip_peer)
        flights["s", i, b, 1] = send(ref.at[span, :], ref.at[span, :], at + 1, core_peer)

    def share_on(i, ref, b):
        at = share_at + 3 * (i * NB + b)
        flights["s", i, b, 0].wait_recv()
        span = own_span(b, lax.rem(c + 2, n_cond))
        flights["s", i, b, 2] = send(ref.at[span, :], ref.at[span, :], at + 2, core_peer)

    def share_end():
        for i in range(2):
            for b in range(NB):
                flights["s", i, b, 1].wait_recv()
                flights["s", i, b, 2].wait_recv()

    r.vg[11:16, :] = jnp.zeros((5, width), F32)
    loads["mw"].wait()
    r.mwb[...] = half(r.mw[...])
    loads["mem0"].wait()
    first = list(range(0, part_samples, 2))
    half_way = len(first) // 2
    for s in first[: half_way - 1]:
        pair_forward(s)
    for name in ("act", "vec", "rw"):
        loads[name].wait()
    r.rwb[:, : 4 * width] = half(r.rw[:, : 4 * width])
    pair_forward(first[half_way - 1])
    r.rwb[:, 4 * width :] = half(r.rw[:, 4 * width :])
    loads["mem1"].wait()
    first_forward(0, first[half_way:])
    load_moments()
    loads["mask"].wait()
    loads["flag"].wait()
    usable_rows()
    cross_forward(0)
    pl.semaphore_wait(barrier, len(friends))
    send_mixed(0)
    loads["mem2"].wait()
    loads["mem3"].wait()
    first_forward(1, list(range(part_samples, samples, 2)))
    cross_forward(1)
    send_mixed(1)
    loads["dw"].wait()
    r.dwb[...] = half(r.dw[...])
    loads["cot"].wait()
    middle(0)
    middle(1)
    up_grads()
    reduce_core("up")
    cross_backward(0)
    send_query_grads(0)
    down_grads()
    reduce_core("down")
    reduce_plane("up")
    cross_backward_pairs(0)
    cross_backward(1)
    send_query_grads(1)
    cross_backward_pairs(1)
    reduce_plane("down")
    pair_grads(0)
    pair_grads(1)
    reduce_core("pair")
    self_backward(0)
    share(0, r.out16, 0)
    self_backward(1)
    row3_grads()
    reduce_core("row3")
    reduce_line("down")
    row1_grads()
    reduce_core("row1")
    reduce_plane("pair")
    row2_grads()
    reduce_core("row2")
    self_backward_rest(0)
    self_backward_rest(1)
    small_core()
    reduce_plane("row3")
    reduce_line("up")
    reduce_plane("row2")
    gather_line("down")
    reduce_line("row3")
    reduce_plane("row1")
    small_plane()
    gather_line("up")
    reduce_line("pair")
    share(1, r.ga16, 1)
    share(1, r.ga16, 0)
    gather_plane("down")
    share(0, r.out16, 1)
    reduce_line("row1")
    gather_line("row3")
    reduce_line("row2")
    small_line()
    share_on(0, r.out16, 0)
    gather_line("pair")
    gather_plane("up")
    gather_line("row1")
    gather_core("down")
    gather_plane("row3")
    share_on(1, r.ga16, 0)
    gather_line("row2")
    gather_plane("pair")
    gather_core("up")
    gather_plane("row1")
    share_on(0, r.out16, 1)
    gather_plane("row2")
    gather_core("row3")
    gather_core("pair")
    share_on(1, r.ga16, 1)
    gather_core("row1")
    gather_core("row2")
    small_end()
    share_end()
    for name in ("m_r", "m_d", "m_p", "a_r", "a_d", "a_p"):
        loads[name].wait()
    for name in layout:
        end_set(name)
    for copy in pending:
        copy.wait_send()


def step_kernel(names, token_count, *refs):
    r = Names()
    for name, ref in zip(names, refs, strict=True):
        setattr(r, name, ref)
    width = r.w_p.shape[0]
    hidden = r.w_d.shape[0]
    keep = 1.0 - (1.0 + STEP) ** (-0.75)
    copies = []

    def store(src, dst):
        copy = pltpu.make_async_copy(src, dst, r.sem.at[len(copies)])
        copy.start()
        copies.append(copy)

    def update(weight, grad, moment, average):
        scaled = grad / token_count
        moment_new = INERTIA * moment + scaled
        weight_new = weight - STEP_RATE * (scaled + INERTIA * moment_new)
        average_new = keep * average + (1.0 - keep) * weight_new
        return moment_new, weight_new, average_new

    def renew(prefix, row, column, first):
        rows = 32
        cols = slice(column, column + width)

        @pl.loop(0, width // rows, unroll=8)
        def _(i):
            at = pl.multiple_of(i * rows, rows)
            grad = wide(r.tot[pl.ds(first + at, rows), :])
            here = pl.ds(row + at, rows)
            old = [getattr(r, kind + "_" + prefix)[here, cols] for kind in "wma"]
            new = update(old[0], grad, old[1], old[2])
            for kind, value in zip("mwa", new):
                getattr(r, prefix + kind)[here, cols] = value

        for kind in "mwa":
            view = (slice(row, row + width), cols)
            store(getattr(r, prefix + kind).at[view], getattr(r, prefix + kind + "_h").at[view])

    pair_first = 2 * hidden + 6 * width
    order = {5: 0, 4: 1, 3: 2, 0: 3, 1: 4, 2: 5}
    blocks = [("d", j * width, 0, hidden + j * width) for j in range(hidden // width)]
    blocks += [("r", 0, (6 + j) * width, j * width) for j in range(hidden // width)]
    blocks += [("r", 0, j * width, 2 * hidden + order[j] * width) for j in range(6)]
    blocks += [("p", 0, j * width, pair_first + j * width) for j in range(2)]

    r.mwb[...] = half(r.w_p[...])
    total_rows = r.dkv.shape[0]
    chunks = 8
    step = total_rows // chunks
    for i in range(chunks):
        for block in blocks[i * len(blocks) // chunks : (i + 1) * len(blocks) // chunks]:
            renew(*block)
        span = pl.ds(i * step, step)
        r.gm[span, :] = nt(r.dkv[span, :], r.mwb[...])
        store(r.gm.at[span, :], r.gm_h.at[span, :])
    r.out[...] = wide(r.out16[...])
    store(r.out, r.out_h)
    r.ga[...] = wide(r.ga16[...])
    store(r.ga, r.ga_h)
    new = update(r.w_v[...], r.vtot[: r.w_v.shape[0], :], r.m_v[...], r.a_v[...])
    for kind, value in zip("mwa", new):
        getattr(r, "v" + kind)[...] = value
        store(getattr(r, "v" + kind), getattr(r, "v" + kind + "_h"))
    for copy in copies:
        copy.wait()


def per_device(
    actions,
    memory,
    patch_flags,
    memory_mask,
    cotangent,
    row_weights,
    memory_weights,
    down_weight,
    vectors,
    row_momentum,
    memory_momentum,
    down_momentum,
    vector_momentum,
    row_average,
    memory_average,
    down_average,
    vector_average,
):
    rows, width = actions.shape
    samples = rows // H
    slots = memory.shape[1]
    hidden = down_weight.shape[0]
    n_cond = lax.axis_size("cond")
    n_dp = lax.axis_size("dp")
    part_rows = rows // NB
    own = part_rows // n_cond
    total = 2 * hidden + 8 * width
    flat = samples * slots
    ins = {
        "act_h": actions,
        "mem_h": memory.reshape(flat, width),
        "mask_h": memory_mask,
        "flag_h": patch_flags.reshape(1, samples),
        "cot_h": cotangent,
        "rw_h": row_weights,
        "mw_h": memory_weights,
        "dw_h": down_weight,
        "vec_h": vectors,
        "m_r_h": row_momentum,
        "m_d_h": down_momentum,
        "m_p_h": memory_momentum,
        "a_r_h": row_average,
        "a_d_h": down_average,
        "a_p_h": memory_average,
    }
    outs = {
        "tot": ((total, width), BF),
        "vtot": ((16, width), F32),
        "dkv": ((flat, 2 * width), BF),
        "out16": ((rows, width), BF),
        "ga16": ((rows, width), BF),
        "rw": (row_weights.shape, F32),
        "dw": (down_weight.shape, F32),
        "mw": (memory_weights.shape, F32),
        "m_r": (row_weights.shape, F32),
        "m_d": (down_weight.shape, F32),
        "m_p": (memory_weights.shape, F32),
        "a_r": (row_weights.shape, F32),
        "a_d": (down_weight.shape, F32),
        "a_p": (memory_weights.shape, F32),
    }

    n_line = n_dp // 2
    biggest = max(16, hidden // 8 // n_line)

    scratch = {
        "act": ((rows, width), F32),
        "vec": (vectors.shape, F32),
        "mem": ((flat, width), BF),
        "mask": (memory_mask.shape, jnp.int32),
        "flag": ((1, samples), jnp.int32),
        "cot": ((rows, width), F32),
        "rwb": (row_weights.shape, BF),
        "mwb": (memory_weights.shape, BF),
        "dwb": (down_weight.shape, BF),
        "blocks": ((256, 256), BF),
        "heads": ((64, 256), F32),
        "heads_b": ((64, 256), BF),
        "a1": ((rows, width), BF),
        "qkv": ((rows, 3 * width), BF),
        "o1": ((rows, width), BF),
        "x1": ((rows, width), F32),
        "a2": ((rows, width), BF),
        "qs": ((rows, width), BF),
        "kv": ((samples, slots, 2 * width), BF),
        "use": ((samples, slots), F32),
        "p": ((samples, 64, slots), BF),
        "ds": ((samples, 64, slots), BF),
        "o_out": ((rows, width), BF),
        "top": ((rows, 128), F32),
        "total": ((rows, 128), F32),
        "st_in": ((NB, n_cond, 16, 128), F32),
        "st_out": ((NB, n_cond, 16, 128), F32),
        "o_in": ((NB, n_cond, own, width), BF),
        "o2": ((NB * own, width), BF),
        "a3": ((NB * own, width), BF),
        "dz": ((NB * own, width), BF),
        "hb": ((NB * own, hidden), BF),
        "du": ((NB * own, hidden), BF),
        "dx2": ((NB * own, width), F32),
        "dx1": ((NB * own, width), F32),
        "dy2": ((NB * own, width), BF),
        "dqc": ((NB * own, width), BF),
        "dy1": ((NB * own, width), BF),
        "dqkv": ((NB * own, 3 * width), BF),
        "do_in": ((rows, width), BF),
        "do_out": ((NB, n_cond, own, width), BF),
        "dl_in": ((NB, n_cond, 8, 128), F32),
        "dl_out": ((NB, n_cond, 8, 128), F32),
        "dl": ((rows, 128), F32),
        "dq_out": ((rows, width), BF),
        "dq_in": ((NB, n_cond, own, width), BF),
        "vg": ((16, width), F32),
        "v2": ((2, 16, width), F32),
        "v4": ((4, 16, width), F32),
        "vz": ((n_line, 16, width), F32),
        "g": ((total, width), BF),
        "gw": ((width, 2 * width), F32),
        "rc": ((total // 2, width), BF),
        "rp": ((3, total // 8, width), BF),
        "ps": ((total // 8, width), BF),
        "rz": ((6 * n_line * biggest, width), BF),
    }
    sems = {
        "load_sem": pltpu.SemaphoreType.DMA((24,)),
        "ssem": pltpu.SemaphoreType.DMA((128,)),
        "rsem": pltpu.SemaphoreType.DMA((128,)),
    }
    whole = pl.BlockSpec(memory_space=pltpu.VMEM)
    far = pl.BlockSpec(memory_space=pltpu.HBM)
    names = list(ins) + list(outs) + list(scratch) + list(sems)
    sizes = (rows, samples, slots, n_cond, n_dp, width)
    made = pl.pallas_call(
        functools.partial(layer_kernel, names, sizes),
        out_shape=[pltpu.VMEM(*v) for v in outs.values()],
        in_specs=[far] * len(ins),
        out_specs=[whole] * len(outs),
        scratch_shapes=[pltpu.VMEM(*v) for v in scratch.values()] + list(sems.values()),
        compiler_params=pltpu.CompilerParams(
            collective_id=0, has_side_effects=True, vmem_limit_bytes=32 * MIB
        ),
        name="layer",
    )(*(pltpu.with_memory_space_constraint(v, pltpu.HBM) for v in ins.values()))

    ins2 = dict(zip(outs, made, strict=True))
    ins2 |= {"w_v": vectors, "m_v": vector_momentum, "a_v": vector_average}
    outs2 = {
        "out": (rows, width),
        "ga": (rows, width),
        "gm": (flat, width),
    }
    for prefix, array in (("r", row_weights), ("p", memory_weights), ("d", down_weight), ("v", vectors)):
        for kind in "mwa":
            outs2[prefix + kind] = array.shape
    renamed = {"rw": "w_r", "dw": "w_d", "mw": "w_p"}
    names2 = [renamed.get(k, k) for k in ins2]
    names2 += [k + "_h" for k in outs2] + list(outs2) + ["mwb", "sem"]
    results = pl.pallas_call(
        functools.partial(step_kernel, names2, float(rows * n_dp)),
        out_shape=[jax.ShapeDtypeStruct(v, F32) for v in outs2.values()],
        in_specs=[whole] * len(ins2),
        out_specs=[far] * len(outs2),
        scratch_shapes=[pltpu.VMEM(v, F32) for v in outs2.values()]
        + [pltpu.VMEM(memory_weights.shape, BF), pltpu.SemaphoreType.DMA((64,))],
        compiler_params=pltpu.CompilerParams(vmem_limit_bytes=26 * MIB),
        name="step",
    )(*ins2.values())
    out, ga, gm = results[:3]
    return (out, ga, gm.reshape(samples, slots, width), *results[3:])


def solution(mesh):
    in_specs = (
        P("dp", None),
        P("dp", "cond", None),
        P("dp", "cond"),
        P("dp", "cond"),
        P("dp", None),
    ) + (P(),) * 12
    out_specs = (P("dp", None), P("dp", None), P("dp", "cond", None)) + (P(),) * 12
    return jax.shard_map(
        per_device, mesh=mesh, in_specs=in_specs, out_specs=out_specs, check_vma=False
    )
```

time: 88.2 us -> 64.8 us (0.73)
  Pallas kernels: 81.6 us -> 63.8 us
  local copies, waits for them, and re-layouts: 5.39 us -> 0.01 us
    pallas_call x1, Pallas kernels: 71.6 us -> 55.7 us  [per_device(): pl.pallas_call(functools.partial(layer_kernel, names, sizes), out_shape=[...]
    unnamed x25 -> x6, local copies, waits for them, and re-layouts: 5.39 us -> 0.01 us
    pallas_call x1, Pallas kernels: 10.1 us -> 8.08 us  [per_device(): pl.pallas_call(functools.partial(step_kernel, names2, float(rows * n_dp))...]
where the time goes in v2:
time: 64.8 us; the launch traced here: 64.6 us
  Pallas kernels  63.8 us (98%)
  between operations  0.87 us (1%)
    pallas_call x1, Pallas kernels, per_device(): pl.pallas_call(functools.partial(layer_kernel, names, sizes), out_shape=[...  55.7 us
    pallas_call x1, Pallas kernels, per_device(): pl.pallas_call(functools.partial(step_kernel, names2, float(rows * n_dp))...  8.08 us

profile of v2, /device:TPU:1, one launch (start us, length us, event | category | flops | bytes accessed | tf_op | source)
XLA Modules:
  0.0 64.6 jit_solution(8084948764704691246)
XLA Ops:
  0.7 0.0 copy-start
  0.7 0.0 copy-start.1
  0.7 0.0 copy-start.2
  0.7 55.7 %layer.1 = (bf16[4096,256]{1,0:T(8,128)(2,1)S(1)}, f32[16,256]{1,0:T(8,128)S(1)}, bf16[6400,512]{1,0:T(8,128)(2,1)S(1)}, bf16[512,256]{1,0:T(8,128)(2,1)S(1)}, b...) custom-call(f32[512,256]{1,0:T(8,128)} %refs_0_.1, ...), custom_call_target="tpu_custom_call" | custom-call | tf_op jit(solution)/shard_map/layer/pallas_call | solution.py:1113
  56.4 0.0 copy-done
  56.4 0.0 copy-done.1
  56.4 0.0 copy-done.2
  56.4 8.1 %step.1 = (f32[512,256]{1,0:T(8,128)}, f32[512,256]{1,0:T(8,128)}, f32[6400,256]{1,0:T(8,128)}, f32[256,2560]{1,0:T(8,128)}, f32[256,2560]{1,0:T(8,128)}, /*inde...) custom-call(bf16[4096,256]{1,0:T(8,128)(2,1)S(1)} %get-tuple-element, ...), custom_call_target="tpu_custom_call" | custom-call | tf_op jit(solution)/shard_map/step/pallas_call | solution.py:1138
Async XLA Ops:
  0.7 55.7 %copy-start = (f32[11,256]{1,0:T(8,128)S(1)}, f32[11,256]{1,0:T(8,128)}, u32[]{:S(2)}) copy-start(f32[11,256]{1,0:T(8,128)} %refs_14_.3) | copy-start | bytes 33796
  0.7 55.7 %copy-start.1 = (f32[11,256]{1,0:T(8,128)S(1)}, f32[11,256]{1,0:T(8,128)}, u32[]{:S(2)}) copy-start(f32[11,256]{1,0:T(8,128)} %refs_15_.1) | copy-start | bytes 33796
  0.7 55.7 %copy-start.2 = (f32[11,256]{1,0:T(8,128)S(1)}, f32[11,256]{1,0:T(8,128)}, u32[]{:S(2)}) copy-start(f32[11,256]{1,0:T(8,128)} %refs_16_.1) | copy-start | bytes 33796

commit v3 on v2

--- a/solution.py
+++ b/solution.py
@@ -144,7 +144,7 @@
     core = lax.rem(c, 2)
     side_x = lax.rem(d, 2)
     side_y = c // 2
-    plane = side_x + 2 * side_y
+    plane = 2 * side_x + side_y
     line = d // 2
     n_line = n_dp // 2
     core_peer = (d, c + 1 - 2 * core)
@@ -153,7 +153,7 @@
     def plane_place(k):
         x = 1 - side_x if k & 1 else side_x
         y = 1 - side_y if k & 2 else side_y
-        return x + 2 * y
+        return 2 * x + y
 
     def plane_peer(k):
         return (
@@ -549,8 +549,7 @@
         "up": (0, hidden),
         "down": (hidden, hidden),
         "row1": (2 * hidden, 2 * width),
-        "row2": (2 * hidden + 2 * width, 2 * width),
-        "row3": (2 * hidden + 4 * width, 2 * width),
+        "row2": (2 * hidden + 2 * width, 4 * width),
         "pair": (pair_first, 2 * width),
     }
     set_at = {name: 5 * NB * n_cond + 10 * i for i, name in enumerate(layout)}
@@ -839,66 +838,60 @@
     reduce_core("up")
     cross_backward(0)
     send_query_grads(0)
+    cross_backward_pairs(0)
+    reduce_plane("up")
     down_grads()
     reduce_core("down")
-    reduce_plane("up")
-    cross_backward_pairs(0)
+    pair_grads(0)
     cross_backward(1)
     send_query_grads(1)
     cross_backward_pairs(1)
     reduce_plane("down")
-    pair_grads(0)
     pair_grads(1)
+    reduce_line("up")
     reduce_core("pair")
     self_backward(0)
-    share(0, r.out16, 0)
+    self_backward_rest(0)
     self_backward(1)
+    reduce_plane("pair")
+    row2_grads()
     row3_grads()
-    reduce_core("row3")
+    reduce_core("row2")
     reduce_line("down")
+    reduce_plane("row2")
     row1_grads()
     reduce_core("row1")
-    reduce_plane("pair")
-    row2_grads()
-    reduce_core("row2")
-    self_backward_rest(0)
-    self_backward_rest(1)
-    small_core()
-    reduce_plane("row3")
-    reduce_line("up")
-    reduce_plane("row2")
-    gather_line("down")
-    reduce_line("row3")
-    reduce_plane("row1")
-    small_plane()
     gather_line("up")
     reduce_line("pair")
+    share(1, r.ga16, 0)
+    share(0, r.out16, 1)
+    self_backward_rest(1)
+    reduce_plane("row1")
+    gather_line("down")
+    small_core()
+    gather_plane("up")
+    reduce_line("row2")
+    small_plane()
+    gather_line("pair")
+    reduce_line("row1")
+    gather_plane("down")
     share(1, r.ga16, 1)
-    share(1, r.ga16, 0)
-    gather_plane("down")
-    share(0, r.out16, 1)
-    reduce_line("row1")
-    gather_line("row3")
-    reduce_line("row2")
+    gather_line("row2")
+    gather_line("row1")
+    share_on(1, r.ga16, 0)
+    gather_core("up")
+    share(0, r.out16, 0)
     small_line()
+    share_on(0, r.out16, 1)
+    gather_plane("pair")
+    gather_plane("row2")
+    share_on(1, r.ga16, 1)
+    gather_core("down")
+    gather_plane("row1")
+    gather_core("pair")
+    gather_core("row2")
     share_on(0, r.out16, 0)
-    gather_line("pair")
-    gather_plane("up")
-    gather_line("row1")
-    gather_core("down")
-    gather_plane("row3")
-    share_on(1, r.ga16, 0)
-    gather_line("row2")
-    gather_plane("pair")
-    gather_core("up")
-    gather_plane("row1")
-    share_on(0, r.out16, 1)
-    gather_plane("row2")
-    gather_core("row3")
-    gather_core("pair")
-    share_on(1, r.ga16, 1)
     gather_core("row1")
-    gather_core("row2")
     small_end()
     share_end()
     for name in ("m_r", "m_d", "m_p", "a_r", "a_d", "a_p"):
@@ -1041,7 +1034,7 @@
     }
 
     n_line = n_dp // 2
-    biggest = max(16, hidden // 8 // n_line)
+    biggest = max(16, hidden // 4 // n_line)
 
     scratch = {
         "act": ((rows, width), F32),

time: 64.8 us -> 62.1 us (0.958)
  Pallas kernels: 63.8 us -> 61.1 us
    pallas_call x1, Pallas kernels: 55.7 us -> 53 us  [per_device(): pl.pallas_call(functools.partial(layer_kernel, names, sizes), out_shape=[...]
where the time goes in v3:
time: 62.1 us; the launch traced here: 62 us
  Pallas kernels  61.1 us (98%)
  between operations  0.87 us (1%)
    pallas_call x1, Pallas kernels, per_device(): pl.pallas_call(functools.partial(layer_kernel, names, sizes), out_shape=[...  53 us
    pallas_call x1, Pallas kernels, per_device(): pl.pallas_call(functools.partial(step_kernel, names2, float(rows * n_dp))...  8.08 us

profile of v3, /device:TPU:1, one launch (start us, length us, event | category | flops | bytes accessed | tf_op | source)
XLA Modules:
  0.0 62.0 jit_solution(13159700386843229068)
XLA Ops:
  0.7 0.0 copy-start
  0.7 0.0 copy-start.1
  0.7 0.0 copy-start.2
  0.7 53.0 %layer.1 = (bf16[4096,256]{1,0:T(8,128)(2,1)S(1)}, f32[16,256]{1,0:T(8,128)S(1)}, bf16[6400,512]{1,0:T(8,128)(2,1)S(1)}, bf16[512,256]{1,0:T(8,128)(2,1)S(1)}, b...) custom-call(f32[512,256]{1,0:T(8,128)} %refs_0_.1, ...), custom_call_target="tpu_custom_call" | custom-call | tf_op jit(solution)/shard_map/layer/pallas_call | solution.py:1106
  53.7 0.0 copy-done
  53.7 0.0 copy-done.1
  53.7 0.0 copy-done.2
  53.8 8.1 %step.1 = (f32[512,256]{1,0:T(8,128)}, f32[512,256]{1,0:T(8,128)}, f32[6400,256]{1,0:T(8,128)}, f32[256,2560]{1,0:T(8,128)}, f32[256,2560]{1,0:T(8,128)}, /*inde...) custom-call(bf16[4096,256]{1,0:T(8,128)(2,1)S(1)} %get-tuple-element, ...), custom_call_target="tpu_custom_call" | custom-call | tf_op jit(solution)/shard_map/step/pallas_call | solution.py:1131
Async XLA Ops:
  0.7 53.1 %copy-start = (f32[11,256]{1,0:T(8,128)S(1)}, f32[11,256]{1,0:T(8,128)}, u32[]{:S(2)}) copy-start(f32[11,256]{1,0:T(8,128)} %refs_14_.3) | copy-start | bytes 33796
  0.7 53.1 %copy-start.1 = (f32[11,256]{1,0:T(8,128)S(1)}, f32[11,256]{1,0:T(8,128)}, u32[]{:S(2)}) copy-start(f32[11,256]{1,0:T(8,128)} %refs_15_.1) | copy-start | bytes 33796
  0.7 53.1 %copy-start.2 = (f32[11,256]{1,0:T(8,128)S(1)}, f32[11,256]{1,0:T(8,128)}, u32[]{:S(2)}) copy-start(f32[11,256]{1,0:T(8,128)} %refs_16_.1) | copy-start | bytes 33796
